TPU v7x, 32 devices: a whole 2x2x4 slice. The times are simulated.
32 devices in a mesh: beam: 2 (over y), chan: 16 (over z, x, core).
Axes of the slice: x: 2, y: 2, z: 4, core: 2. Of those that a mesh axis runs over, the one named last changes fastest.
Arguments:
- filterbank: bfloat16 [2048, 4096], P(('beam', 'chan')), parts along dimension 0
- shift_table: int32 [511], replicated, may hold values from 0 to 511, as said below
- box_widths: int32 [8], replicated, may hold values from 1 to 255, as said below
Outputs:
- dedispersed: bfloat16 [512, 4096], P(('beam', 'chan')), parts along dimension 0
- peaks: float32 [16, 256], P('beam', 'chan'), parts along dimension 0
There are 2 independent parts, one for each index of `beam`. A program takes and returns all parts, laid end to end along the dimension named above; an argument that names none is the same for every part. Nothing has to cross between parts.
Inputs may be any that keep to these rules, and one draw needn't show every extreme that they name: `shift_table`: entry k - 1 + j, for k a power of two up to 256 and j < k, is the delay for merged trial j of a section with k trials; it equals 2 j or 2 j + 1. `box_widths`: entry i lies between 2**i and 2**(i+1) - 1.
All inputs are finite; a program needn't handle non-finite values.
Results may differ from a plain program's by a relative error of at most 0.001.
Values sent between devices are 32-bit elements; how exact they have to be, the bound alone decides.
A program may use at most 64 MiB of HBM per device.

v0:
```python
import jax
import jax.numpy as jnp
from jax import lax
from jax.sharding import PartitionSpec as P

ROWS = 16


epsilon = 1e-05


def swapped(block, axis, bit):
    count = lax.axis_size(axis)
    route = []
    for low in range(count):
        high = low | 1 << bit
        if high != low and high < count:
            route += [(low, high), (high, low)]
    return lax.ppermute(block, axis, route)


def advance(rows_in, shifts, start):
    length = rows_in.shape[-1]
    count = rows_in.shape[-2]
    leading = rows_in.shape[:-2]
    last_axis = rows_in.ndim - 1
    padded = jnp.concatenate([rows_in, jnp.zeros_like(rows_in)], axis=last_axis)
    base = jnp.minimum(2 * start, length)
    moved = lax.dynamic_slice_in_dim(padded, base, length, last_axis)
    width = length + 2 * count
    wide = jnp.concatenate(
        [moved, jnp.zeros(leading + (count, 2 * count), moved.dtype)], axis=last_axis
    )
    flat = wide.reshape(leading + (count * width,))
    flat = jnp.concatenate(
        [flat, jnp.zeros(leading + (2 * count,), moved.dtype)], axis=last_axis - 1
    )
    skewed = flat.reshape(leading + (count, width + 2))[..., :length]
    odd_moved = jnp.concatenate(
        [skewed[..., 1:], jnp.zeros(leading + (count, 1), moved.dtype)], axis=last_axis
    )
    parity = shifts - 2 * (start + jnp.arange(count, dtype=jnp.int32))
    return jnp.where((parity == 1)[:, None], odd_moved, skewed)


def merge_pairs(subbands, shift_table, trials_now):
    paired = subbands.reshape(subbands.shape[0] // 2, 2, subbands.shape[1], subbands.shape[2])
    lower_rows = paired[:, 0]
    upper_rows = paired[:, 1]
    if trials_now > subbands.shape[1]:
        lower_rows = jnp.repeat(lower_rows, 2, axis=1)
        upper_rows = jnp.repeat(upper_rows, 2, axis=1)
    return lower_rows + advance(upper_rows, shift_table[trials_now - 1 : 2 * trials_now - 1], 0)


def local_tree(spectra, shift_table):
    chan_count = spectra.shape[0]
    subbands = spectra[:, None, :]
    band_span = 1
    while band_span < chan_count:
        band_span *= 2
        subbands = merge_pairs(subbands, shift_table, max(1, band_span * ROWS // chan_count))
    return subbands[0]


def flat_tree(channel_mean, shift_table, chan_count):
    subband = channel_mean[None, :]
    band_span = 1
    while band_span < chan_count:
        band_span *= 2
        trials_now = max(1, band_span * ROWS // chan_count)
        if trials_now > subband.shape[0]:
            subband = jnp.repeat(subband, 2, axis=0)
        subband = subband + advance(subband, shift_table[trials_now - 1 : 2 * trials_now - 1], 0)
    return subband


def normalize(channel_block):
    values = channel_block.astype(jnp.float32)
    centre = jnp.mean(values, axis=1, keepdims=True)
    spread = jnp.mean(jnp.square(values - centre), axis=1, keepdims=True)
    return (values - centre) * lax.rsqrt(spread + epsilon)


def boxcar_peaks(scaled, box_widths):
    length = scaled.shape[1]
    running = jnp.cumsum(scaled, axis=1)
    padded = jnp.concatenate([jnp.zeros_like(running), running], axis=1)

    def single(box_width):
        earlier = lax.dynamic_slice_in_dim(padded, length - box_width, length, 1)
        box_sums = (running - earlier) * lax.rsqrt(box_width.astype(jnp.float32))
        return jnp.max(box_sums, axis=1)

    return lax.map(single, box_widths)


def shards(filterbank, shift_table, box_widths):
    chan_count = filterbank.shape[0]
    half_rows = ROWS // 2
    section_count = lax.axis_size("chan").bit_length() - 1
    normal = normalize(filterbank)
    partial_value = jnp.sum(normal, axis=0)
    current = local_tree(normal, shift_table)
    device_index = lax.axis_index("chan")
    position = jnp.zeros((), jnp.int32)
    for bit_number in range(section_count):
        upper_side = device_index >> bit_number & 1
        trials_now = 2 * ROWS * (1 << bit_number)
        payload = jnp.concatenate([current, partial_value[None, :]], axis=0)
        arrived = swapped(payload, "chan", bit_number)
        received = arrived[:ROWS]
        partial_value = partial_value + arrived[ROWS]
        lower_all = jnp.where(upper_side == 0, current, received)
        upper_all = jnp.where(upper_side == 0, received, current)
        lower_rows = lax.dynamic_slice_in_dim(lower_all, upper_side * half_rows, half_rows, 0)
        upper_rows = lax.dynamic_slice_in_dim(upper_all, upper_side * half_rows, half_rows, 0)
        first_trial = 2 * (position * ROWS + upper_side * half_rows)
        shifts = lax.dynamic_slice_in_dim(shift_table, trials_now - 1 + first_trial, ROWS)
        current = jnp.repeat(lower_rows, 2, axis=0) + advance(
            jnp.repeat(upper_rows, 2, axis=0), shifts, first_trial
        )
        position = 2 * position + upper_side
    channel_mean = partial_value / (chan_count * lax.axis_size("chan"))
    mean_rows = flat_tree(channel_mean, shift_table, chan_count)
    place = jnp.zeros((), jnp.int32)
    for bit_number in range(section_count):
        side = device_index >> bit_number & 1
        trials_now = 2 * ROWS * (1 << bit_number)
        mean_half = lax.dynamic_slice_in_dim(mean_rows, side * half_rows, half_rows, 0)
        first_trial = 2 * (place * ROWS + side * half_rows)
        shifts = lax.dynamic_slice_in_dim(shift_table, trials_now - 1 + first_trial, ROWS)
        doubled = jnp.repeat(mean_half, 2, axis=0)
        mean_rows = doubled + advance(doubled, shifts, first_trial)
        place = 2 * place + side
    current = current - mean_rows
    centre = jnp.mean(current, axis=1, keepdims=True)
    spread = jnp.mean(jnp.square(current - centre), axis=1, keepdims=True)
    scaled = (current - centre) * lax.rsqrt(spread + epsilon)
    dedispersed = scaled.astype(jnp.bfloat16)
    peaks = boxcar_peaks(scaled, box_widths)
    return (dedispersed, peaks)


def solution(mesh):
    placed = (P(("beam", "chan"), None), P(), P())
    return jax.shard_map(
        shards,
        mesh=mesh,
        in_specs=placed,
        out_specs=(P(("beam", "chan"), None), P("beam", "chan")),
        check_vma=False,
    )
```

profile of v0, /device:TPU:0, one launch (start us, length us, event | category | flops | bytes accessed | tf_op | source)
XLA Modules:
  0.0 118.3 jit_solution(13654196649057623181)
XLA Ops:
  0.7 1.3 %slice.229 = s32[1]{0:T(128)} slice(s32[511]{0:T(512)} %param.6), slice={[0:1]} | slice | bytes 8 | tf_op jit(solution)/shard_map/slice | solution.py:53
  1.9 0.8 subtract_compare_fusion.7
  2.8 1.2 %convert_reduce_fusion = f32[64]{0:T(128)S(1)} fusion(bf16[64,4096]{1,0:T(8,128)(2,1)} %param.5), kind=kLoop, calls=%fused_computation.2 | loop fusion | flops 524224 | bytes 524544 | tf_op jit(solution)/shard_map/reduce_sum | solution.py:80
  4.1 0.3 fusion.2
  4.6 0.6 reshape_broadcast_in_dim.3
  5.2 0.6 slice.296
  5.8 0.3 copy.31
  6.2 0.4 reshape.282
  6.6 1.2 slice.297
  8.4 0.8 fusion.3
  9.8 0.3 reshape.286
  10.9 0.3 slice.305
  13.9 0.4 reshape.299
  14.4 0.3 reshape.300
  15.6 0.4 reshape.302
  16.0 0.7 pad_reduce_fusion
  17.4 0.5 collective-permute-start
  17.9 1.3 %collective-permute-done = f32[17,4096]{1,0:T(8,128)S(1)} collective-permute-done((f32[17,4096]{1,0:T(8,128)S(1)}, f32[17,4096]{1,0:T(8,128)S(1)}, u32[]{:S(2)}, u32[]{:S(2)}) %collective-permute-start) | collective-permute-done | bytes 278560 | tf_op jit(solution)/shard_map/ppermute | solution.py:19
  20.9 2.9 %collective-permute-start.1 = (f32[17,4096]{1,0:T(8,128)S(1)}, f32[17,4096]{1,0:T(8,128)S(1)}, u32[]{:S(2)}, u32[]{:S(2)}) collective-permute-start(f32[17,4096]{1,0:T(8,128)S(1)} %pad_maximum_fusion.1), channel_id=1, source_target_pairs={{0,2},{2,0},{1,3},{3,1},{4,6},{6,4},{5,7},{7,5},{8,10},{10,8},{9,1... | collective-permute-start | bytes 835592 | tf_op jit(solution)/shard_map/ppermute | solution.py:19
  23.8 9.4 %collective-permute-done.1 = f32[17,4096]{1,0:T(8,128)S(1)} collective-permute-done((f32[17,4096]{1,0:T(8,128)S(1)}, f32[17,4096]{1,0:T(8,128)S(1)}, u32[]{:S(2)}, u32[]{:S(2)}) %collective-permute-start.1) | collective-permute-done | bytes 278560 | tf_op jit(solution)/shard_map/ppermute | solution.py:19
  34.8 1.9 %collective-permute-start.2 = (f32[17,4096]{1,0:T(8,128)S(1)}, f32[17,4096]{1,0:T(8,128)S(1)}, u32[]{:S(2)}, u32[]{:S(2)}) collective-permute-start(f32[17,4096]{1,0:T(8,128)S(1)} %pad_maximum_fusion.2), channel_id=1, source_target_pairs={{0,4},{4,0},{1,5},{5,1},{2,6},{6,2},{3,7},{7,3},{8,12},{12,8},{9,1... | collective-permute-start | bytes 835592 | tf_op jit(solution)/shard_map/ppermute | solution.py:19
  36.6 8.8 %collective-permute-done.2 = f32[17,4096]{1,0:T(8,128)S(1)} collective-permute-done((f32[17,4096]{1,0:T(8,128)S(1)}, f32[17,4096]{1,0:T(8,128)S(1)}, u32[]{:S(2)}, u32[]{:S(2)}) %collective-permute-start.2) | collective-permute-done | bytes 278560 | tf_op jit(solution)/shard_map/ppermute | solution.py:19
  47.0 2.6 %collective-permute-start.3 = (f32[17,4096]{1,0:T(8,128)S(1)}, f32[17,4096]{1,0:T(8,128)S(1)}, u32[]{:S(2)}, u32[]{:S(2)}) collective-permute-start(f32[17,4096]{1,0:T(8,128)S(1)} %pad_maximum_fusion.3), channel_id=1, source_target_pairs={{0,8},{8,0},{1,9},{9,1},{2,10},{10,2},{3,11},{11,3},{4,12},{12,4},... | collective-permute-start | bytes 835592 | tf_op jit(solution)/shard_map/ppermute | solution.py:19
  49.9 16.2 %collective-permute-done.3 = f32[17,4096]{1,0:T(8,128)S(1)} collective-permute-done((f32[17,4096]{1,0:T(8,128)S(1)}, f32[17,4096]{1,0:T(8,128)S(1)}, u32[]{:S(2)}, u32[]{:S(2)}) %collective-permute-start.3) | collective-permute-done | bytes 278560 | tf_op jit(solution)/shard_map/ppermute | solution.py:19
  72.2 0.7 copy-done.1
  73.0 0.9 slice-done
  76.3 0.3 fusion.32
  76.8 0.8 multiply_bitcast_fusion
  77.6 4.6 %reduce-window.6 = f32[16,32,128]{2,1,0:T(8,128)S(1)} reduce-window(f32[16,32,128]{2,1,0:T(8,128)S(1)} %bitcast.76, f32[]{:T(128)} %constant.50.clone.1), window={size=1x1x128 pad=0_0x0_0x127_0}, to_apply=%region_5.6 | reduce-window | flops 8323072 | bytes 524292 | tf_op jit(solution)/shard_map/reduce-window
  82.2 0.3 slice_reduce_fusion
  83.0 0.6 copy-done.3
  83.6 34.6 %while.12 = (s32[]{:T(128)}, f32[8,16]{1,0:T(8,128)}, s32[8]{0:T(128)S(1)}, f32[16,8192]{1,0:T(8,128)S(1)}, f32[16,4096]{1,0:T(8,128)S(1)}, /*index=5*/s32[]{:T(128)}, s32[1]{0:T(128)}, s32[]{:T(128)}, s32[1]{0:T(128)}) while((s32[]{:T(128)}, f32[8,16]{1,0:T(8,128)}, s32[8]{0:T(128)S(1)}, f32[16,8192]{1,0:T(8,128)S(1)}, ...), condition=%wide.region_9.10_spmd, body=%wide.region_7.9_spmd.sunk | while | flops 196599 | bytes 524667 | solution.py:95
  83.6 0.7 dynamic_slice.201
  86.7 1.3 %dynamic_update_slice.8 = f32[8,16]{1,0:T(8,128)} dynamic-update-slice(f32[8,16]{1,0:T(8,128)} %get-tuple-element.149, f32[1,16]{1,0:T(1,128)S(1)} %bitcast.85, s32[]{:T(128)S(6)} %copy.38, s32[]{:T(128)} %constant.48.clone.1..sunk) | dynamic-update-slice | bytes 132 | tf_op jit(solution)/shard_map/while/body/jit(dynamic_update_index_in_dim)/dynamic_update_slice | solution.py:95
  88.0 0.7 dynamic_slice.201
  91.0 1.3 %dynamic_update_slice.8 = f32[8,16]{1,0:T(8,128)} dynamic-update-slice(f32[8,16]{1,0:T(8,128)} %get-tuple-element.149, f32[1,16]{1,0:T(1,128)S(1)} %bitcast.85, s32[]{:T(128)S(6)} %copy.38, s32[]{:T(128)} %constant.48.clone.1..sunk) | dynamic-update-slice | bytes 132 | tf_op jit(solution)/shard_map/while/body/jit(dynamic_update_index_in_dim)/dynamic_update_slice | solution.py:95
  92.3 0.7 dynamic_slice.201
  95.3 1.3 %dynamic_update_slice.8 = f32[8,16]{1,0:T(8,128)} dynamic-update-slice(f32[8,16]{1,0:T(8,128)} %get-tuple-element.149, f32[1,16]{1,0:T(1,128)S(1)} %bitcast.85, s32[]{:T(128)S(6)} %copy.38, s32[]{:T(128)} %constant.48.clone.1..sunk) | dynamic-update-slice | bytes 132 | tf_op jit(solution)/shard_map/while/body/jit(dynamic_update_index_in_dim)/dynamic_update_slice | solution.py:95
  96.6 0.7 dynamic_slice.201
  99.7 1.3 %dynamic_update_slice.8 = f32[8,16]{1,0:T(8,128)} dynamic-update-slice(f32[8,16]{1,0:T(8,128)} %get-tuple-element.149, f32[1,16]{1,0:T(1,128)S(1)} %bitcast.85, s32[]{:T(128)S(6)} %copy.38, s32[]{:T(128)} %constant.48.clone.1..sunk) | dynamic-update-slice | bytes 132 | tf_op jit(solution)/shard_map/while/body/jit(dynamic_update_index_in_dim)/dynamic_update_slice | solution.py:95
  101.0 0.7 dynamic_slice.201
  104.0 1.3 %dynamic_update_slice.8 = f32[8,16]{1,0:T(8,128)} dynamic-update-slice(f32[8,16]{1,0:T(8,128)} %get-tuple-element.149, f32[1,16]{1,0:T(1,128)S(1)} %bitcast.85, s32[]{:T(128)S(6)} %copy.38, s32[]{:T(128)} %constant.48.clone.1..sunk) | dynamic-update-slice | bytes 132 | tf_op jit(solution)/shard_map/while/body/jit(dynamic_update_index_in_dim)/dynamic_update_slice | solution.py:95
  105.3 0.7 dynamic_slice.201
  108.3 1.3 %dynamic_update_slice.8 = f32[8,16]{1,0:T(8,128)} dynamic-update-slice(f32[8,16]{1,0:T(8,128)} %get-tuple-element.149, f32[1,16]{1,0:T(1,128)S(1)} %bitcast.85, s32[]{:T(128)S(6)} %copy.38, s32[]{:T(128)} %constant.48.clone.1..sunk) | dynamic-update-slice | bytes 132 | tf_op jit(solution)/shard_map/while/body/jit(dynamic_update_index_in_dim)/dynamic_update_slice | solution.py:95
  109.6 0.7 dynamic_slice.201
  112.7 1.3 %dynamic_update_slice.8 = f32[8,16]{1,0:T(8,128)} dynamic-update-slice(f32[8,16]{1,0:T(8,128)} %get-tuple-element.149, f32[1,16]{1,0:T(1,128)S(1)} %bitcast.85, s32[]{:T(128)S(6)} %copy.38, s32[]{:T(128)} %constant.48.clone.1..sunk) | dynamic-update-slice | bytes 132 | tf_op jit(solution)/shard_map/while/body/jit(dynamic_update_index_in_dim)/dynamic_update_slice | solution.py:95
  114.0 0.7 dynamic_slice.201
  117.0 1.3 %dynamic_update_slice.8 = f32[8,16]{1,0:T(8,128)} dynamic-update-slice(f32[8,16]{1,0:T(8,128)} %get-tuple-element.149, f32[1,16]{1,0:T(1,128)S(1)} %bitcast.85, s32[]{:T(128)S(6)} %copy.38, s32[]{:T(128)} %constant.48.clone.1..sunk) | dynamic-update-slice | bytes 132 | tf_op jit(solution)/shard_map/while/body/jit(dynamic_update_index_in_dim)/dynamic_update_slice | solution.py:95
  (217 shorter events, 21.0 us)
Async XLA Ops:
  0.6 2.0 %copy-start.2 = (s32[511]{0:T(512)S(1)}, s32[511]{0:T(512)}, u32[]{:S(2)}) copy-start(s32[511]{0:T(512)} %param.6) | copy-start | bytes 6136
  0.6 3.4 %copy-start = (bf16[64,4096]{1,0:T(8,128)(2,1)S(1)}, bf16[64,4096]{1,0:T(8,128)(2,1)}, u32[]{:S(2)}) copy-start(bf16[64,4096]{1,0:T(8,128)(2,1)} %param.5) | copy-start | bytes 1572868
  17.4 1.9 %collective-permute-start = (f32[17,4096]{1,0:T(8,128)S(1)}, f32[17,4096]{1,0:T(8,128)S(1)}, u32[]{:S(2)}, u32[]{:S(2)}) collective-permute-start(f32[17,4096]{1,0:T(8,128)S(1)} %pad_maximum_fusion), channel_id=1, source_target_pairs={{0,1},{1,0},{2,3},{3,2},{4,5},{5,4},{6,7},{7,6},{8,9},{9,8},{10,11... | collective-permute-start | bytes 835592 | tf_op jit(solution)/shard_map/ppermute | solution.py:19
  20.9 12.3 %collective-permute-start.1 = (f32[17,4096]{1,0:T(8,128)S(1)}, f32[17,4096]{1,0:T(8,128)S(1)}, u32[]{:S(2)}, u32[]{:S(2)}) collective-permute-start(f32[17,4096]{1,0:T(8,128)S(1)} %pad_maximum_fusion.1), channel_id=1, source_target_pairs={{0,2},{2,0},{1,3},{3,1},{4,6},{6,4},{5,7},{7,5},{8,10},{10,8},{9,1... | collective-permute-start | bytes 835592 | tf_op jit(solution)/shard_map/ppermute | solution.py:19
  34.8 10.7 %collective-permute-start.2 = (f32[17,4096]{1,0:T(8,128)S(1)}, f32[17,4096]{1,0:T(8,128)S(1)}, u32[]{:S(2)}, u32[]{:S(2)}) collective-permute-start(f32[17,4096]{1,0:T(8,128)S(1)} %pad_maximum_fusion.2), channel_id=1, source_target_pairs={{0,4},{4,0},{1,5},{5,1},{2,6},{6,2},{3,7},{7,3},{8,12},{12,8},{9,1... | collective-permute-start | bytes 835592 | tf_op jit(solution)/shard_map/ppermute | solution.py:19
  47.0 19.1 %collective-permute-start.3 = (f32[17,4096]{1,0:T(8,128)S(1)}, f32[17,4096]{1,0:T(8,128)S(1)}, u32[]{:S(2)}, u32[]{:S(2)}) collective-permute-start(f32[17,4096]{1,0:T(8,128)S(1)} %pad_maximum_fusion.3), channel_id=1, source_target_pairs={{0,8},{8,0},{1,9},{9,1},{2,10},{10,2},{3,11},{11,3},{4,12},{12,4},... | collective-permute-start | bytes 835592 | tf_op jit(solution)/shard_map/ppermute | solution.py:19
  72.2 0.7 copy-start.1
  73.0 1.0 slice-start
  83.0 0.7 copy-start.3
where the time goes:
time: 119 us; the launch traced here: 118 us
  local copies, waits for them, and re-layouts  40.6 us (34%)
  waiting for transfers between devices  35.8 us (30%)
  loops' own time  16.9 us (14%)
  other arithmetic  14.1 us (12%)
  starting transfers between devices  7.92 us (7%)
  between operations  2.95 us (2%)
    ppermute x4, waiting for transfers between devices, swapped(): return lax.ppermute(block, axis, route)  35.8 us
    another operation x1, loops' own time, boxcar_peaks(): return lax.map(single, box_widths)  16.9 us
    dynamic_update_slice x8, local copies, waits for them, and re-layouts, boxcar_peaks(): return lax.map(single, box_widths)  10.4 us
    ppermute x4, starting transfers between devices, swapped(): return lax.ppermute(block, axis, route)  7.92 us
    dynamic_slice x8, local copies, waits for them, and re-layouts, boxcar_peaks(): return lax.map(single, box_widths)  5.3 us
    another operation x4, other arithmetic  4.95 us
    slice x20, local copies, waits for them, and re-layouts, advance(): skewed[..., 1:]  3.63 us
    reshape x20, local copies, waits for them, and re-layouts, advance(): skewed = flat.reshape(leading + (count, width + 2))[..., :length]  3.42 us
  transfers between devices with their start and end apart: 4, of which 4 were waited for; matrix products, arithmetic and copies ran while one was open for 0% of the time, Pallas kernels for 0%

commit v1 on v0

v1 whole, which is shorter than its diff:
```python
import functools

import jax
import jax.numpy as jnp
from jax import lax
from jax.experimental import pallas as pl
from jax.experimental.pallas import tpu as pltpu
from jax.sharding import PartitionSpec as P

ROWS = 16
SUB = 8
LANES = 128
GROUP_BITS = 4

epsilon = 1e-05

VMEM_LIMIT = 48 * 1024 * 1024


def lane_index():
    return lax.broadcasted_iota(jnp.int32, (SUB, LANES), 1)


def next_sublane(tile):
    sub = lax.broadcasted_iota(jnp.int32, tile.shape, tile.ndim - 2)
    return jnp.where(sub == SUB - 1, 0.0, pltpu.roll(tile, SUB - 1, tile.ndim - 2))


def combine(tiles, amount):
    back = (LANES - amount) & (LANES - 1)
    turned = [pltpu.roll(tile, back, tile.ndim - 1) for tile in tiles]
    lane = lax.broadcasted_iota(jnp.int32, tiles[0].shape, tiles[0].ndim - 1)
    keep = lane < LANES - amount
    return [jnp.where(keep, turned[i], turned[i + 1]) for i in range(len(tiles) - 1)]


def advanced(tiles, amount):
    return combine(list(tiles) + [next_sublane(tiles[0])], amount)


def plus(first, second):
    return [a + b for a, b in zip(first, second)]


def digit_bits(digit, bits):
    return [(digit // (1 << i)) % 2 for i in range(bits)]


def partner(bit_values, k):
    flipped = [1 - b if k >> i & 1 else b for i, b in enumerate(bit_values)]
    plain = sum((b * (1 << i) for i, b in enumerate(flipped)), 0)
    turned = sum((b * (1 << len(flipped) - 1 - i) for i, b in enumerate(flipped)), 0)
    return plain, turned


def peer_rounds(bits):
    return sorted(range(1, 1 << bits), reverse=True)


def enter(peers):
    barrier = pltpu.get_barrier_semaphore()
    for peer in peers:
        pl.semaphore_signal(
            barrier, inc=1, device_id={"chan": peer}, device_id_type=pl.DeviceIdType.MESH
        )
    return barrier


def remote(src, dst, send_sem, recv_sem, k, peer):
    return pltpu.make_async_remote_copy(
        src_ref=src,
        dst_ref=dst,
        send_sem=send_sem.at[k],
        recv_sem=recv_sem.at[k],
        device_id={"chan": peer},
        device_id_type=pl.DeviceIdType.MESH,
    )


def front_kernel(
    bits, total_channels, fb, table, rows, mean_row,
    norm, base, level2, level4, level8, send, pieces, landed, gathered,
    scat_send, scat_recv, gath_send, gath_recv, row_send, row_recv, own_sem,
):
    group = 1 << bits
    held = ROWS // group
    channels, length = fb.shape
    wide = length // SUB
    count = wide // LANES
    me = lax.axis_index("chan")
    digit = me % group
    mine = digit_bits(digit, bits)
    _, my_turn = partner(mine, 0)
    rounds = peer_rounds(bits)
    peers = {}
    for k in rounds:
        plain, turned = partner(mine, k)
        peers[k] = (me - digit + plain, plain, turned)
    barrier = enter([peers[k][0] for k in rounds])

    step = 16
    for first in range(0, channels, step):
        values = fb[first : first + step, :].astype(jnp.float32)
        centre = jnp.mean(values, axis=1, keepdims=True)
        moved = values - centre
        spread = jnp.mean(jnp.square(moved), axis=1, keepdims=True)
        scaled = moved * lax.rsqrt(spread + epsilon)
        for s in range(SUB):
            for m in range(count):
                at = s * wide + m * LANES
                norm[m, pl.ds(first * SUB + s, step, stride=SUB), :] = scaled[:, at : at + LANES]

    single = table[0]

    def four(q, partial):
        row = []
        for c in range(4):
            at = pl.multiple_of((4 * q + c) * SUB, SUB)
            row.append([norm[m, pl.ds(at, SUB), :] for m in range(count)])
        summed = plus(plus(row[0], row[1]), plus(row[2], row[3]))
        low = plus(row[0], advanced(row[1], single))
        high = plus(row[2], advanced(row[3], single))
        merged = plus(low, advanced(high, single))
        for m in range(count):
            base[q, :, m * LANES : (m + 1) * LANES] = merged[m]
        return tuple(plus(partial, summed))

    partial = lax.fori_loop(
        0, channels // 4, four, tuple(jnp.zeros((SUB, LANES), jnp.float32) for _ in range(count)), unroll=2
    )
    for e in range(ROWS):
        s, m = 2 * (e // count), e % count
        pieces[e] = partial[m][s : s + 2, :]

    if rounds:
        pl.semaphore_wait(barrier, len(rounds))
    scatter = {}
    for k in rounds:
        chan, plain, turned = peers[k]
        scatter[k] = remote(
            pieces.at[pl.ds(plain * held, held)], landed.at[digit], scat_send, scat_recv, k, chan
        )
        scatter[k].start()

    def tiles_of(load):
        return [load(slice(m * LANES, (m + 1) * LANES)) for m in range(count)]

    subs = channels // 4
    view = base.reshape(subs // 2, 2, 1, SUB, wide)
    trials = 1
    for target in (level2, level4, level8, send):
        trials *= 2
        subs //= 2
        for i in range(trials):
            low = tiles_of(lambda w: view[:, 0, i // 2, :, w])
            high = tiles_of(lambda w: view[:, 1, i // 2, :, w])
            merged = plus(low, advanced(high, table[trials - 1 + i]))
            for m in range(count):
                w = slice(m * LANES, (m + 1) * LANES)
                if subs > 1:
                    target[:, i, :, w] = merged[m]
                else:
                    target[i, :, w] = merged[m][0]
        if subs > 1:
            view = target.reshape(subs // 2, 2, trials, SUB, wide)

    copies = {}
    for k in rounds:
        chan, plain, turned = peers[k]
        copies[k] = remote(
            send.at[pl.ds(turned * held, held)], rows.at[pl.ds(digit * held, held)], row_send, row_recv, k, chan
        )
        copies[k].start()
    own = pltpu.make_async_copy(
        send.at[pl.ds(my_turn * held, held)], rows.at[pl.ds(digit * held, held)], own_sem
    )
    own.start()

    total = pieces[pl.ds(digit * held, held)]
    for k in rounds:
        scatter[k].wait_recv()
        total = total + landed[peers[k][1]]
    gathered[pl.ds(digit * held, held)] = total * (1.0 / total_channels)
    gather = {}
    for k in rounds:
        here = gathered.at[pl.ds(digit * held, held)]
        gather[k] = remote(here, here, gath_send, gath_recv, k, peers[k][0])
        gather[k].start()
    for k in rounds:
        gather[k].wait_recv()
    mean = []
    for m in range(count):
        mean.append(jnp.concatenate([gathered[a * count + m] for a in range(SUB // 2)], axis=0))

    for j in range(held):
        trial = my_turn * held + j
        line = plus(mean, advanced(mean, single))
        line = plus(line, advanced(line, single))
        for level in range(1, 5):
            now = trial // (1 << 4 - level)
            line = plus(line, advanced(line, table[(1 << level) - 1 + now]))
        for m in range(count):
            mean_row[j, :, m * LANES : (m + 1) * LANES] = line[m]

    own.wait()
    for k in rounds:
        copies[k].wait_recv()
    for k in rounds:
        scatter[k].wait_send()
        gather[k].wait_send()
        copies[k].wait_send()


def front(filterbank, shift_table, bits, total_channels):
    channels, length = filterbank.shape
    wide = length // SUB
    group = 1 << bits
    held = ROWS // group
    f32 = jnp.float32
    return pl.pallas_call(
        functools.partial(front_kernel, bits, total_channels),
        out_shape=(
            jax.ShapeDtypeStruct((ROWS, SUB, wide), f32),
            jax.ShapeDtypeStruct((held, SUB, wide), f32),
        ),
        in_specs=[pl.BlockSpec(memory_space=pltpu.VMEM), pl.BlockSpec(memory_space=pltpu.SMEM)],
        out_specs=(pl.BlockSpec(memory_space=pl.ANY), pl.BlockSpec(memory_space=pltpu.VMEM)),
        scratch_shapes=[
            pltpu.VMEM((wide // LANES, channels * SUB, LANES), f32),
            pltpu.VMEM((16, SUB, wide), f32),
            pltpu.VMEM((8, 2, SUB, wide), f32),
            pltpu.VMEM((4, 4, SUB, wide), f32),
            pltpu.VMEM((2, 8, SUB, wide), f32),
            pltpu.VMEM((ROWS, SUB, wide), f32),
            pltpu.VMEM((ROWS, 2, LANES), f32),
            pltpu.VMEM((group, held, 2, LANES), f32),
            pltpu.VMEM((ROWS, 2, LANES), f32),
        ]
        + [pltpu.SemaphoreType.DMA((group,))] * 6
        + [pltpu.SemaphoreType.DMA],
        compiler_params=pltpu.CompilerParams(
            collective_id=0, has_side_effects=True, vmem_limit_bytes=VMEM_LIMIT
        ),
    )(filterbank, shift_table)


def exchange_kernel(bits, stride, block, rows, row_send, row_recv, own_sem):
    group = 1 << bits
    held = ROWS // group
    me = lax.axis_index("chan")
    digit = (me // stride) % group
    mine = digit_bits(digit, bits)
    _, my_turn = partner(mine, 0)
    rounds = peer_rounds(bits)
    peers = {}
    for k in rounds:
        plain, turned = partner(mine, k)
        peers[k] = (me + (plain - digit) * stride, turned)
    barrier = enter([peers[k][0] for k in rounds])
    pl.semaphore_wait(barrier, len(rounds))
    there = rows.at[pl.ds(digit * held, held)]
    copies = {}
    for k in rounds:
        chan, turned = peers[k]
        copies[k] = remote(block.at[pl.ds(turned * held, held)], there, row_send, row_recv, k, chan)
        copies[k].start()
    own = pltpu.make_async_copy(block.at[pl.ds(my_turn * held, held)], there, own_sem)
    own.start()
    own.wait()
    for k in rounds:
        copies[k].wait()


def exchange(block, bits, stride, number):
    group = 1 << bits
    return pl.pallas_call(
        functools.partial(exchange_kernel, bits, stride),
        out_shape=jax.ShapeDtypeStruct(block.shape, block.dtype),
        in_specs=[pl.BlockSpec(memory_space=pltpu.VMEM)],
        out_specs=pl.BlockSpec(memory_space=pl.ANY),
        scratch_shapes=[pltpu.SemaphoreType.DMA((group,))] * 2 + [pltpu.SemaphoreType.DMA],
        compiler_params=pltpu.CompilerParams(
            collective_id=number, has_side_effects=True, vmem_limit_bytes=VMEM_LIMIT
        ),
    )(block)


def merge_rows(bits, merged, largest, block, correction, table, position, levels):
    group = 1 << bits
    held = ROWS // group
    wide = block.shape[-1]
    count = wide // LANES
    sub = lax.broadcasted_iota(jnp.int32, (SUB, LANES), 0)

    def put(level, row, tiles, is_upper):
        for m in range(count):
            levels[level, row, :, m * LANES : (m + 1) * LANES] = tiles[m]
            if is_upper:
                levels[level, row, :, wide + m * LANES : wide + (m + 1) * LANES] = next_sublane(tiles[m])

    for row in range(ROWS):
        tiles = []
        for m in range(count):
            w = slice(m * LANES, (m + 1) * LANES)
            tile = block[row, :, w]
            tiles.append(tile if correction is None else tile - correction[row % held, :, w])
        put(0, row, tiles, row // held % 2 == 1)
    place = position[0]
    trials = held
    for level in range(bits):
        now = 2 * trials
        whole = merged * ROWS << level + 1
        for i in range(now):
            shift = table[whole - 1 + place * now + i]
            within = shift & (wide - 1)
            at = within // LANES
            for q in range(ROWS // now):
                low = 2 * q * trials + i // 2
                high = low + trials
                tiles = [
                    levels[level, high, :, pl.ds(pl.multiple_of((at + m) * LANES, LANES), LANES)]
                    for m in range(count + 1)
                ]
                moved = combine(tiles, within & (LANES - 1))
                if largest >= wide:
                    up = jnp.minimum(shift // wide, SUB)
                    moved = [
                        jnp.where(sub < SUB - up, pltpu.roll(tile, (SUB - up) & (SUB - 1), 0), 0.0)
                        for tile in moved
                    ]
                lower = [levels[level, low, :, m * LANES : (m + 1) * LANES] for m in range(count)]
                put(level + 1, q * now + i, plus(lower, moved), level + 1 < bits and q % 2 == 1)
        trials = now


def middle_kernel(bits, merged, largest, corrected, position, table, block, *rest):
    correction = rest[0] if corrected else None
    out, levels = rest[-2:]
    merge_rows(bits, merged, largest, block, correction, table, position, levels)
    for row in range(ROWS):
        out[row] = levels[bits, row, :, : block.shape[-1]]


def back_kernel(bits, merged, largest, corrected, position, table, widths, block, *rest):
    correction = rest[0] if corrected else None
    dedispersed, peaks, levels, flat = rest[-4:]
    wide = block.shape[-1]
    length = wide * SUB
    merge_rows(bits, merged, largest, block, correction, table, position, levels)
    for row in range(ROWS):
        for m in range(wide // LANES):
            flat[m, row * SUB : (row + 1) * SUB, :] = levels[bits, row, :, m * LANES : (m + 1) * LANES]
    series = [
        jnp.concatenate([flat[m, pl.ds(s, ROWS, stride=SUB), :] for m in range(wide // LANES)], axis=1)
        for s in range(SUB)
    ]
    summed = series[0]
    for part in series[1:]:
        summed = summed + part
    centre = jnp.sum(summed, axis=1, keepdims=True) * (1.0 / length)
    series = [part - centre for part in series]
    squared = jnp.square(series[0])
    for part in series[1:]:
        squared = squared + jnp.square(part)
    spread = jnp.sum(squared, axis=1, keepdims=True) * (1.0 / length)
    factor = lax.rsqrt(spread + epsilon)
    series = [part * factor for part in series]
    for s in range(SUB):
        dedispersed[:, s * wide : (s + 1) * wide] = series[s].astype(jnp.bfloat16)

    piece = 2 * LANES
    stacked = jnp.concatenate(
        [part[:, a : a + piece] for part in series for a in range(0, wide, piece)], axis=0
    )
    triangle = jnp.where(
        lax.broadcasted_iota(jnp.int32, (piece, piece), 0) <= lax.broadcasted_iota(jnp.int32, (piece, piece), 1),
        1.0,
        0.0,
    ).astype(jnp.bfloat16)
    rest_value = stacked
    inner = None
    for _ in range(3):
        top = rest_value.astype(jnp.bfloat16)
        rest_value = rest_value - top.astype(jnp.float32)
        product = jnp.dot(top, triangle, preferred_element_type=jnp.float32)
        inner = product if inner is None else inner + product
    offset = jnp.zeros((ROWS, 1), jnp.float32)
    prefix = []
    for p in range(length // piece):
        one = inner[p * ROWS : (p + 1) * ROWS, :] + offset
        offset = one[:, piece - 1 : piece]
        prefix += [one[:, :LANES], one[:, LANES:]]

    lane = lax.broadcasted_iota(jnp.int32, (ROWS, LANES), 1)
    diagonal = lane == lax.broadcasted_iota(jnp.int32, (ROWS, LANES), 0)
    zero = jnp.zeros((ROWS, LANES), jnp.float32)
    count = peaks.shape[0]
    for i in range(count):
        width = widths[i]
        whole, amount = divmod(1 << i, LANES)
        amount = width - whole * LANES
        keep = lane >= amount
        best = None
        before = zero
        for c in range(len(prefix)):
            source = c - whole
            now = pltpu.roll(prefix[source], amount, 1) if source >= 0 else zero
            box = prefix[c] - jnp.where(keep, now, before)
            before = now
            best = box if best is None else jnp.maximum(best, box)
        root = lax.rsqrt(jnp.full((ROWS, 1), width, jnp.int32).astype(jnp.float32))
        column = jnp.max(best, axis=1, keepdims=True) * root
        line = jnp.sum(jnp.where(diagonal, column, 0.0), axis=0, keepdims=True)
        peaks[i : i + 1, :] = line[:, :ROWS]


def merge(block, correction, shift_table, position, bits, merged, box_widths):
    wide = block.shape[-1]
    largest = 2 * ((merged * ROWS << bits) - 1) + 1
    corrected = correction is not None
    smem = pl.BlockSpec(memory_space=pltpu.SMEM)
    vmem = pl.BlockSpec(memory_space=pltpu.VMEM)
    levels = pltpu.VMEM((bits + 1, ROWS, SUB, 2 * wide), jnp.float32)
    params = pltpu.CompilerParams(vmem_limit_bytes=VMEM_LIMIT)
    data = (block, correction) if corrected else (block,)
    if box_widths is None:
        return pl.pallas_call(
            functools.partial(middle_kernel, bits, merged, largest, corrected),
            out_shape=jax.ShapeDtypeStruct(block.shape, jnp.float32),
            in_specs=[smem] * 2 + [vmem] * len(data),
            out_specs=vmem,
            scratch_shapes=[levels],
            compiler_params=params,
        )(position, shift_table, *data)
    return pl.pallas_call(
        functools.partial(back_kernel, bits, merged, largest, corrected),
        out_shape=(
            jax.ShapeDtypeStruct((ROWS, SUB * wide), jnp.bfloat16),
            jax.ShapeDtypeStruct((box_widths.shape[0], ROWS), jnp.float32),
        ),
        in_specs=[smem] * 3 + [vmem] * len(data),
        out_specs=(vmem, vmem),
        scratch_shapes=[levels, pltpu.VMEM((wide // LANES, ROWS * SUB, LANES), jnp.float32)],
        compiler_params=params,
    )(position, shift_table, box_widths, *data)


def shards(filterbank, shift_table, box_widths):
    devices = lax.axis_size("chan")
    all_bits = devices.bit_length() - 1
    me = lax.axis_index("chan")
    bits = min(GROUP_BITS, all_bits)
    rows, correction = front(filterbank, shift_table, bits, filterbank.shape[0] * devices)
    for bit in range(bits, all_bits):
        route = [(source, source ^ 1 << bit) for source in range(devices)]
        correction = correction + lax.ppermute(correction, "chan", route)
    done = 0
    position = jnp.zeros((), jnp.int32)
    while True:
        for bit in range(done, done + bits):
            position = 2 * position + (me >> bit & 1)
        last = done + bits == all_bits
        result = merge(
            rows, correction, shift_table, position[None], bits, 1 << done, box_widths if last else None
        )
        if last:
            return result
        done += bits
        bits = min(GROUP_BITS, all_bits - done)
        rows = exchange(result, bits, 1 << done, done)
        correction = None


def solution(mesh):
    placed = (P(("beam", "chan"), None), P(), P())
    return jax.shard_map(
        shards,
        mesh=mesh,
        in_specs=placed,
        out_specs=(P(("beam", "chan"), None), P("beam", "chan")),
        check_vma=False,
    )
```

time: 119 us -> 27.2 us (0.23)
  local copies, waits for them, and re-layouts: 40.6 us -> 2.37 us
  waiting for transfers between devices: 35.8 us -> 0 us
  Pallas kernels: 0 us -> 23.9 us
  loops' own time: 16.9 us -> 0 us
  other arithmetic: 14.1 us -> 0 us
  starting transfers between devices: 7.92 us -> 0 us
  between operations: 2.95 us -> 0.67 us
    ppermute x4 -> x0, waiting for transfers between devices: 35.8 us -> none  [swapped(): return lax.ppermute(block, axis, route)]
    pallas_call x0 -> x2, Pallas kernels: none -> 23.9 us  [the longest x1 16.3 us: front(): pl.pallas_call(functools.partial(front_kernel, bits, total_channels), out...]
    another operation x1 -> x0, loops' own time: 16.9 us -> none  [boxcar_peaks(): return lax.map(single, box_widths)]
    dynamic_update_slice x8 -> x0, local copies, waits for them, and re-layouts: 10.4 us -> none  [boxcar_peaks(): return lax.map(single, box_widths)]
    reshape x58 -> x0, local copies, waits for them, and re-layouts: 9.94 us -> none  [the longest x20 3.42 us: advance(): skewed = flat.reshape(leading + (count, width + 2))[..., :length]]
    ppermute x4 -> x0, starting transfers between devices: 7.92 us -> none  [swapped(): return lax.ppermute(block, axis, route)]
    slice x34 -> x0, local copies, waits for them, and re-layouts: 6.81 us -> none  [the longest x20 3.63 us: advance(): skewed[..., 1:]]
    dynamic_slice x20 -> x0, local copies, waits for them, and re-layouts: 6.69 us -> none  [the longest x8 5.3 us: boxcar_peaks(): return lax.map(single, box_widths)]
  transfers between devices with their start and end apart: 4 -> 0, of which waited for: 4 -> 0; matrix products, arithmetic and copies ran while one was open for 0% -> 0% of each run, Pallas kernels for 0% -> 0%
where the time goes in v1:
time: 27.2 us; the launch traced here: 27 us
  Pallas kernels  23.9 us (88%)
  local copies, waits for them, and re-layouts  2.37 us (9%)
  between operations  0.67 us (2%)
    pallas_call x1, Pallas kernels, front(): pl.pallas_call(functools.partial(front_kernel, bits, total_channels), out...  16.3 us
    pallas_call x1, Pallas kernels, merge(): pl.pallas_call(functools.partial(back_kernel, bits, merged, largest, corr...  7.64 us
    unnamed x6, local copies, waits for them, and re-layouts  2.37 us

profile of v1, /device:TPU:0, one launch (start us, length us, event | category | flops | bytes accessed | tf_op | source)
XLA Modules:
  0.0 27.0 jit_solution(3641478341285572518)
XLA Ops:
  0.6 0.0 copy-start.1
  0.7 0.7 %copy-done.1 = s32[511]{0:T(512)S(1)} copy-done((s32[511]{0:T(512)S(1)}, s32[511]{0:T(512)}, u32[]{:S(2)}) %copy-start.1) | copy-done | bytes 2068
  1.3 0.0 copy-start
  1.3 1.0 %copy-done = bf16[64,4096]{1,0:T(8,128)(2,1)S(1)} copy-done((bf16[64,4096]{1,0:T(8,128)(2,1)S(1)}, bf16[64,4096]{1,0:T(8,128)(2,1)}, u32[]{:S(2)}) %copy-start) | copy-done | bytes 524312
  2.4 16.3 %shard_map.50 = (f32[16,8,512]{2,1,0:T(8,128)S(1)}, f32[1,8,512]{2,1,0:T(8,128)S(1)}) custom-call(bf16[64,4096]{1,0:T(8,128)(2,1)S(1)} %copy-done, s32[511]{0:T(512)S(1)} %copy-done.1), custom_call_target="tpu_custom_call" | custom-call | tf_op jit(solution)/shard_map/pallas_call | solution.py:220
  18.7 0.0 copy-start.2
  18.7 0.6 %copy-done.2 = s32[8]{0:T(128)S(1)} copy-done((s32[8]{0:T(128)S(1)}, s32[8]{0:T(128)}, u32[]{:S(2)}) %copy-start.2) | copy-done | bytes 56
  19.3 7.6 %shard_map.51 = (bf16[16,4096]{1,0:T(8,128)(2,1)}, f32[8,16]{1,0:T(8,128)}) custom-call(s32[1]{0:T(128)} %bitcast.position, s32[511]{0:T(512)S(1)} %copy-done.1, s32[8]{0:T(128)S(1)} %copy-done.2, f32[16,8,512]{2,1,0:T(8,128)S(1)} %get-tuple-element.4.block, f32[1,8,512]{2,1,0:T(8,128)S(1)} %get-tuple-element.5.rest_0_), custom_call_target="tpu_custom_call" | custom-call | tf_op jit(solution)/shard_map/pallas_call | solution.py:435
Async XLA Ops:
  0.6 0.7 %copy-start.1 = (s32[511]{0:T(512)S(1)}, s32[511]{0:T(512)}, u32[]{:S(2)}) copy-start(s32[511]{0:T(512)} %table.3) | copy-start | bytes 6136
  1.3 1.0 %copy-start = (bf16[64,4096]{1,0:T(8,128)(2,1)S(1)}, bf16[64,4096]{1,0:T(8,128)(2,1)}, u32[]{:S(2)}) copy-start(bf16[64,4096]{1,0:T(8,128)(2,1)} %fb.1) | copy-start | bytes 1572868
  18.7 0.7 %copy-start.2 = (s32[8]{0:T(128)S(1)}, s32[8]{0:T(128)}, u32[]{:S(2)}) copy-start(s32[8]{0:T(128)} %widths.1) | copy-start | bytes 100

commit v2 on v1

--- a/solution.py
+++ b/solution.py
@@ -78,8 +78,8 @@
 
 
 def front_kernel(
-    bits, total_channels, fb, table, rows, mean_row,
-    norm, base, level2, level4, level8, send, pieces, landed, gathered,
+    bits, total_channels, fb_far, table_far, rows, mean_row,
+    fb, table, in_sem, table_sem, norm, base, level2, level4, level8, send, pieces, landed, gathered,
     scat_send, scat_recv, gath_send, gath_recv, row_send, row_recv, own_sem,
 ):
     group = 1 << bits
@@ -87,6 +87,15 @@
     channels, length = fb.shape
     wide = length // SUB
     count = wide // LANES
+    step = 16
+    arrivals = []
+    for n, first in enumerate(range(0, channels, step)):
+        block = pl.ds(first, step)
+        arrivals.append(pltpu.make_async_copy(fb_far.at[block], fb.at[block], in_sem.at[n]))
+    table_in = pltpu.make_async_copy(table_far, table, table_sem)
+    for arrival in arrivals:
+        arrival.start()
+    table_in.start()
     me = lax.axis_index("chan")
     digit = me % group
     mine = digit_bits(digit, bits)
@@ -98,8 +107,8 @@
         peers[k] = (me - digit + plain, plain, turned)
     barrier = enter([peers[k][0] for k in rounds])
 
-    step = 16
-    for first in range(0, channels, step):
+    for arrival, first in zip(arrivals, range(0, channels, step)):
+        arrival.wait()
         values = fb[first : first + step, :].astype(jnp.float32)
         centre = jnp.mean(values, axis=1, keepdims=True)
         moved = values - centre
@@ -110,24 +119,21 @@
                 at = s * wide + m * LANES
                 norm[m, pl.ds(first * SUB + s, step, stride=SUB), :] = scaled[:, at : at + LANES]
 
+    table_in.wait()
     single = table[0]
-
-    def four(q, partial):
+    partial = None
+    for q in range(channels // 4):
         row = []
         for c in range(4):
-            at = pl.multiple_of((4 * q + c) * SUB, SUB)
-            row.append([norm[m, pl.ds(at, SUB), :] for m in range(count)])
+            at = (4 * q + c) * SUB
+            row.append([norm[m, at : at + SUB, :] for m in range(count)])
         summed = plus(plus(row[0], row[1]), plus(row[2], row[3]))
+        partial = summed if partial is None else plus(partial, summed)
         low = plus(row[0], advanced(row[1], single))
         high = plus(row[2], advanced(row[3], single))
         merged = plus(low, advanced(high, single))
         for m in range(count):
             base[q, :, m * LANES : (m + 1) * LANES] = merged[m]
-        return tuple(plus(partial, summed))
-
-    partial = lax.fori_loop(
-        0, channels // 4, four, tuple(jnp.zeros((SUB, LANES), jnp.float32) for _ in range(count)), unroll=2
-    )
     for e in range(ROWS):
         s, m = 2 * (e // count), e % count
         pieces[e] = partial[m][s : s + 2, :]
@@ -223,9 +229,13 @@
             jax.ShapeDtypeStruct((ROWS, SUB, wide), f32),
             jax.ShapeDtypeStruct((held, SUB, wide), f32),
         ),
-        in_specs=[pl.BlockSpec(memory_space=pltpu.VMEM), pl.BlockSpec(memory_space=pltpu.SMEM)],
+        in_specs=[pl.BlockSpec(memory_space=pltpu.HBM)] * 2,
         out_specs=(pl.BlockSpec(memory_space=pl.ANY), pl.BlockSpec(memory_space=pltpu.VMEM)),
         scratch_shapes=[
+            pltpu.VMEM(filterbank.shape, filterbank.dtype),
+            pltpu.SMEM(shift_table.shape, shift_table.dtype),
+            pltpu.SemaphoreType.DMA((channels // 16,)),
+            pltpu.SemaphoreType.DMA,
             pltpu.VMEM((wide // LANES, channels * SUB, LANES), f32),
             pltpu.VMEM((16, SUB, wide), f32),
             pltpu.VMEM((8, 2, SUB, wide), f32),
@@ -285,7 +295,7 @@
     )(block)
 
 
-def merge_rows(bits, merged, largest, block, correction, table, position, levels):
+def merge_rows(bits, merged, largest, block, correction, table_in, table, place, levels, keep):
     group = 1 << bits
     held = ROWS // group
     wide = block.shape[-1]
@@ -293,10 +303,13 @@
     sub = lax.broadcasted_iota(jnp.int32, (SUB, LANES), 0)
 
     def put(level, row, tiles, is_upper):
+        if level == bits:
+            keep(row, tiles)
+            return
         for m in range(count):
-            levels[level, row, :, m * LANES : (m + 1) * LANES] = tiles[m]
+            levels[level][row, :, m * LANES : (m + 1) * LANES] = tiles[m]
             if is_upper:
-                levels[level, row, :, wide + m * LANES : wide + (m + 1) * LANES] = next_sublane(tiles[m])
+                levels[level][row, :, wide + m * LANES : wide + (m + 1) * LANES] = next_sublane(tiles[m])
 
     for row in range(ROWS):
         tiles = []
@@ -305,20 +318,23 @@
             tile = block[row, :, w]
             tiles.append(tile if correction is None else tile - correction[row % held, :, w])
         put(0, row, tiles, row // held % 2 == 1)
-    place = position[0]
+    table_in.wait()
     trials = held
     for level in range(bits):
         now = 2 * trials
         whole = merged * ROWS << level + 1
-        for i in range(now):
-            shift = table[whole - 1 + place * now + i]
-            within = shift & (wide - 1)
-            at = within // LANES
-            for q in range(ROWS // now):
+        source = levels[level]
+        pairs = [(q, i) for i in range(now) for q in range(ROWS // now)]
+        for first in range(0, ROWS, 8):
+            made = []
+            for q, i in pairs[first : first + 8]:
+                shift = table[whole - 1 + place * now + i]
+                within = shift & (wide - 1)
+                at = within // LANES
                 low = 2 * q * trials + i // 2
                 high = low + trials
                 tiles = [
-                    levels[level, high, :, pl.ds(pl.multiple_of((at + m) * LANES, LANES), LANES)]
+                    source[high, :, pl.ds(pl.multiple_of((at + m) * LANES, LANES), LANES)]
                     for m in range(count + 1)
                 ]
                 moved = combine(tiles, within & (LANES - 1))
@@ -328,28 +344,51 @@
                         jnp.where(sub < SUB - up, pltpu.roll(tile, (SUB - up) & (SUB - 1), 0), 0.0)
                         for tile in moved
                     ]
-                lower = [levels[level, low, :, m * LANES : (m + 1) * LANES] for m in range(count)]
-                put(level + 1, q * now + i, plus(lower, moved), level + 1 < bits and q % 2 == 1)
+                lower = [source[low, :, m * LANES : (m + 1) * LANES] for m in range(count)]
+                made.append((q * now + i, plus(lower, moved), q % 2 == 1))
+            for row, tiles, is_upper in made:
+                put(level + 1, row, tiles, is_upper)
         trials = now
 
 
-def middle_kernel(bits, merged, largest, corrected, position, table, block, *rest):
+def stage_position(merged, bits):
+    me = lax.axis_index("chan")
+    known = merged.bit_length() - 1 + bits
+    return partner(digit_bits(me, known), 0)[1]
+
+
+def middle_kernel(bits, merged, largest, corrected, table_far, block, *rest):
     correction = rest[0] if corrected else None
-    out, levels = rest[-2:]
-    merge_rows(bits, merged, largest, block, correction, table, position, levels)
-    for row in range(ROWS):
-        out[row] = levels[bits, row, :, : block.shape[-1]]
-
-
-def back_kernel(bits, merged, largest, corrected, position, table, widths, block, *rest):
+    out, table, table_sem = rest[corrected : corrected + 3]
+    levels = rest[corrected + 3 :]
+    table_in = pltpu.make_async_copy(table_far, table, table_sem)
+    table_in.start()
+
+    def keep(row, tiles):
+        for m in range(len(tiles)):
+            out[row, :, m * LANES : (m + 1) * LANES] = tiles[m]
+
+    place = stage_position(merged, bits)
+    merge_rows(bits, merged, largest, block, correction, table_in, table, place, levels, keep)
+
+
+def back_kernel(bits, merged, largest, corrected, table_far, widths_far, block, *rest):
     correction = rest[0] if corrected else None
-    dedispersed, peaks, levels, flat = rest[-4:]
+    dedispersed, peaks, flat, widths, widths_sem, table, table_sem = rest[corrected : corrected + 7]
+    levels = rest[corrected + 7 :]
     wide = block.shape[-1]
     length = wide * SUB
-    merge_rows(bits, merged, largest, block, correction, table, position, levels)
-    for row in range(ROWS):
-        for m in range(wide // LANES):
-            flat[m, row * SUB : (row + 1) * SUB, :] = levels[bits, row, :, m * LANES : (m + 1) * LANES]
+    table_in = pltpu.make_async_copy(table_far, table, table_sem)
+    widths_in = pltpu.make_async_copy(widths_far, widths, widths_sem)
+    table_in.start()
+    widths_in.start()
+
+    def keep(row, tiles):
+        for m in range(len(tiles)):
+            flat[m, row * SUB : (row + 1) * SUB, :] = tiles[m]
+
+    place = stage_position(merged, bits)
+    merge_rows(bits, merged, largest, block, correction, table_in, table, place, levels, keep)
     series = [
         jnp.concatenate([flat[m, pl.ds(s, ROWS, stride=SUB), :] for m in range(wide // LANES)], axis=1)
         for s in range(SUB)
@@ -373,7 +412,8 @@
         [part[:, a : a + piece] for part in series for a in range(0, wide, piece)], axis=0
     )
     triangle = jnp.where(
-        lax.broadcasted_iota(jnp.int32, (piece, piece), 0) <= lax.broadcasted_iota(jnp.int32, (piece, piece), 1),
+        lax.broadcasted_iota(jnp.int32, (piece, piece + LANES), 0)
+        <= lax.broadcasted_iota(jnp.int32, (piece, piece + LANES), 1),
         1.0,
         0.0,
     ).astype(jnp.bfloat16)
@@ -384,17 +424,18 @@
         rest_value = rest_value - top.astype(jnp.float32)
         product = jnp.dot(top, triangle, preferred_element_type=jnp.float32)
         inner = product if inner is None else inner + product
-    offset = jnp.zeros((ROWS, 1), jnp.float32)
+    offset = jnp.zeros((ROWS, LANES), jnp.float32)
     prefix = []
     for p in range(length // piece):
-        one = inner[p * ROWS : (p + 1) * ROWS, :] + offset
-        offset = one[:, piece - 1 : piece]
-        prefix += [one[:, :LANES], one[:, LANES:]]
+        one = inner[p * ROWS : (p + 1) * ROWS, :]
+        prefix += [one[:, :LANES] + offset, one[:, LANES:piece] + offset]
+        offset = offset + one[:, piece:]
 
     lane = lax.broadcasted_iota(jnp.int32, (ROWS, LANES), 1)
     diagonal = lane == lax.broadcasted_iota(jnp.int32, (ROWS, LANES), 0)
     zero = jnp.zeros((ROWS, LANES), jnp.float32)
     count = peaks.shape[0]
+    widths_in.wait()
     for i in range(count):
         width = widths[i]
         whole, amount = divmod(1 << i, LANES)
@@ -414,55 +455,51 @@
         peaks[i : i + 1, :] = line[:, :ROWS]
 
 
-def merge(block, correction, shift_table, position, bits, merged, box_widths):
+def merge(block, correction, shift_table, bits, merged, box_widths):
     wide = block.shape[-1]
     largest = 2 * ((merged * ROWS << bits) - 1) + 1
     corrected = correction is not None
-    smem = pl.BlockSpec(memory_space=pltpu.SMEM)
+    far = pl.BlockSpec(memory_space=pltpu.HBM)
     vmem = pl.BlockSpec(memory_space=pltpu.VMEM)
-    levels = pltpu.VMEM((bits + 1, ROWS, SUB, 2 * wide), jnp.float32)
+    levels = [pltpu.VMEM((ROWS, SUB, 2 * wide), jnp.float32)] * bits
+    table = [pltpu.SMEM(shift_table.shape, shift_table.dtype), pltpu.SemaphoreType.DMA]
     params = pltpu.CompilerParams(vmem_limit_bytes=VMEM_LIMIT)
     data = (block, correction) if corrected else (block,)
     if box_widths is None:
         return pl.pallas_call(
             functools.partial(middle_kernel, bits, merged, largest, corrected),
             out_shape=jax.ShapeDtypeStruct(block.shape, jnp.float32),
-            in_specs=[smem] * 2 + [vmem] * len(data),
+            in_specs=[far] + [vmem] * len(data),
             out_specs=vmem,
-            scratch_shapes=[levels],
+            scratch_shapes=table + levels,
             compiler_params=params,
-        )(position, shift_table, *data)
+        )(shift_table, *data)
+    widths = [pltpu.SMEM(box_widths.shape, box_widths.dtype), pltpu.SemaphoreType.DMA]
     return pl.pallas_call(
         functools.partial(back_kernel, bits, merged, largest, corrected),
         out_shape=(
             jax.ShapeDtypeStruct((ROWS, SUB * wide), jnp.bfloat16),
             jax.ShapeDtypeStruct((box_widths.shape[0], ROWS), jnp.float32),
         ),
-        in_specs=[smem] * 3 + [vmem] * len(data),
+        in_specs=[far] * 2 + [vmem] * len(data),
         out_specs=(vmem, vmem),
-        scratch_shapes=[levels, pltpu.VMEM((wide // LANES, ROWS * SUB, LANES), jnp.float32)],
+        scratch_shapes=[pltpu.VMEM((wide // LANES, ROWS * SUB, LANES), jnp.float32)] + widths + table + levels,
         compiler_params=params,
-    )(position, shift_table, box_widths, *data)
+    )(shift_table, box_widths, *data)
 
 
 def shards(filterbank, shift_table, box_widths):
     devices = lax.axis_size("chan")
     all_bits = devices.bit_length() - 1
-    me = lax.axis_index("chan")
     bits = min(GROUP_BITS, all_bits)
     rows, correction = front(filterbank, shift_table, bits, filterbank.shape[0] * devices)
     for bit in range(bits, all_bits):
         route = [(source, source ^ 1 << bit) for source in range(devices)]
         correction = correction + lax.ppermute(correction, "chan", route)
     done = 0
-    position = jnp.zeros((), jnp.int32)
     while True:
-        for bit in range(done, done + bits):
-            position = 2 * position + (me >> bit & 1)
         last = done + bits == all_bits
-        result = merge(
-            rows, correction, shift_table, position[None], bits, 1 << done, box_widths if last else None
-        )
+        result = merge(rows, correction, shift_table, bits, 1 << done, box_widths if last else None)
         if last:
             return result
         done += bits

time: 27.2 us -> 23.4 us (0.86)
  Pallas kernels: 23.9 us -> 20.2 us
    pallas_call x1, Pallas kernels: 7.64 us -> 3.58 us  [merge(): pl.pallas_call(functools.partial(back_kernel, bits, merged, largest, corr...]
    pallas_call x1, Pallas kernels: 16.3 us -> 16.6 us  [front(): pl.pallas_call(functools.partial(front_kernel, bits, total_channels), out...]
where the time goes in v2:
time: 23.4 us; the launch traced here: 23.2 us
  Pallas kernels  20.2 us (86%)
  local copies, waits for them, and re-layouts  2.37 us (10%)
  between operations  0.66 us (3%)
    pallas_call x1, Pallas kernels, front(): pl.pallas_call(functools.partial(front_kernel, bits, total_channels), out...  16.6 us
    pallas_call x1, Pallas kernels, merge(): pl.pallas_call(functools.partial(back_kernel, bits, merged, largest, corr...  3.58 us
    unnamed x6, local copies, waits for them, and re-layouts  2.37 us

profile of v2, /device:TPU:0, one launch (start us, length us, event | category | flops | bytes accessed | tf_op | source)
XLA Modules:
  0.0 23.2 jit_solution(16339467615937183882)
XLA Ops:
  0.6 0.0 copy-start
  0.6 1.0 %copy-done = bf16[64,4096]{1,0:T(8,128)(2,1)S(1)} copy-done((bf16[64,4096]{1,0:T(8,128)(2,1)S(1)}, bf16[64,4096]{1,0:T(8,128)(2,1)}, u32[]{:S(2)}) %copy-start) | copy-done | bytes 524312
  1.7 0.0 copy-start.1
  1.7 0.7 %copy-done.1 = s32[511]{0:T(512)S(1)} copy-done((s32[511]{0:T(512)S(1)}, s32[511]{0:T(512)}, u32[]{:S(2)}) %copy-start.1) | copy-done | bytes 2068
  2.4 16.6 %shard_map.50 = (f32[16,8,512]{2,1,0:T(8,128)S(1)}, f32[1,8,512]{2,1,0:T(8,128)S(1)}) custom-call(bf16[64,4096]{1,0:T(8,128)(2,1)S(1)} %copy-done, s32[511]{0:T(512)S(1)} %copy-done.1), custom_call_target="tpu_custom_call" | custom-call | tf_op jit(solution)/shard_map/pallas_call | solution.py:226
  19.0 0.0 copy-start.2
  19.0 0.6 %copy-done.2 = s32[8]{0:T(128)S(1)} copy-done((s32[8]{0:T(128)S(1)}, s32[8]{0:T(128)}, u32[]{:S(2)}) %copy-start.2) | copy-done | bytes 56
  19.6 3.6 %shard_map.51 = (bf16[16,4096]{1,0:T(8,128)(2,1)}, f32[8,16]{1,0:T(8,128)}) custom-call(s32[511]{0:T(512)S(1)} %copy-done.1, s32[8]{0:T(128)S(1)} %copy-done.2, f32[16,8,512]{2,1,0:T(8,128)S(1)} %get-tuple-element.4.block, f32[1,8,512]{2,1,0:T(8,128)S(1)} %get-tuple-element.5.rest_0_), custom_call_target="tpu_custom_call" | custom-call | tf_op jit(solution)/shard_map/pallas_call | solution.py:478
Async XLA Ops:
  0.6 1.0 %copy-start = (bf16[64,4096]{1,0:T(8,128)(2,1)S(1)}, bf16[64,4096]{1,0:T(8,128)(2,1)}, u32[]{:S(2)}) copy-start(bf16[64,4096]{1,0:T(8,128)(2,1)} %fb_far.1) | copy-start | bytes 1572868
  1.7 0.7 %copy-start.1 = (s32[511]{0:T(512)S(1)}, s32[511]{0:T(512)}, u32[]{:S(2)}) copy-start(s32[511]{0:T(512)} %table_far.3) | copy-start | bytes 6136
  19.0 0.7 %copy-start.2 = (s32[8]{0:T(128)S(1)}, s32[8]{0:T(128)}, u32[]{:S(2)}) copy-start(s32[8]{0:T(128)} %widths_far.1) | copy-start | bytes 100

commit v3 on v2

--- a/solution.py
+++ b/solution.py
@@ -78,9 +78,22 @@
 
 
 def front_kernel(
-    bits, total_channels, fb_far, table_far, rows, mean_row,
-    fb, table, in_sem, table_sem, norm, base, level2, level4, level8, send, pieces, landed, gathered,
-    scat_send, scat_recv, gath_send, gath_recv, row_send, row_recv, own_sem,
+    bits, total_channels, whole, fb_far, table_far, widths_far, *rest,
+):
+    if whole:
+        dedispersed, peaks, rows, mean_row, flat, *rest = rest
+    else:
+        rows, mean_row, *rest = rest
+    front_steps(
+        bits, total_channels, fb_far, table_far, widths_far, rows, mean_row,
+        (dedispersed, peaks, flat) if whole else None, *rest
+    )
+
+
+def front_steps(
+    bits, total_channels, fb_far, table_far, widths_far, rows, mean_row, ending,
+    widths, widths_sem, fb, table, in_sem, table_sem, norm, base, level2, level4, level8, send, pieces, landed, gathered,
+    scat_send, scat_recv, gath_send, gath_recv, row_send, row_recv, own_sem, *levels,
 ):
     group = 1 << bits
     held = ROWS // group
@@ -96,6 +109,9 @@
     for arrival in arrivals:
         arrival.start()
     table_in.start()
+    if ending:
+        widths_in = pltpu.make_async_copy(widths_far, widths, widths_sem)
+        widths_in.start()
     me = lax.axis_index("chan")
     digit = me % group
     mine = digit_bits(digit, bits)
@@ -119,34 +135,35 @@
                 at = s * wide + m * LANES
                 norm[m, pl.ds(first * SUB + s, step, stride=SUB), :] = scaled[:, at : at + LANES]
 
+    partial = None
+    for c in range(channels):
+        row = [norm[m, c * SUB : (c + 1) * SUB, :] for m in range(count)]
+        partial = row if partial is None else plus(partial, row)
+    for e in range(ROWS):
+        s, m = 2 * (e // count), e % count
+        pieces[e] = partial[m][s : s + 2, :]
+    if rounds:
+        pl.semaphore_wait(barrier, len(rounds))
+    scatter = {}
+    for k in rounds:
+        chan, plain, turned = peers[k]
+        scatter[k] = remote(
+            pieces.at[pl.ds(plain * held, held)], landed.at[digit], scat_send, scat_recv, k, chan
+        )
+        scatter[k].start()
+
     table_in.wait()
     single = table[0]
-    partial = None
     for q in range(channels // 4):
         row = []
         for c in range(4):
             at = (4 * q + c) * SUB
             row.append([norm[m, at : at + SUB, :] for m in range(count)])
-        summed = plus(plus(row[0], row[1]), plus(row[2], row[3]))
-        partial = summed if partial is None else plus(partial, summed)
         low = plus(row[0], advanced(row[1], single))
         high = plus(row[2], advanced(row[3], single))
         merged = plus(low, advanced(high, single))
         for m in range(count):
             base[q, :, m * LANES : (m + 1) * LANES] = merged[m]
-    for e in range(ROWS):
-        s, m = 2 * (e // count), e % count
-        pieces[e] = partial[m][s : s + 2, :]
-
-    if rounds:
-        pl.semaphore_wait(barrier, len(rounds))
-    scatter = {}
-    for k in rounds:
-        chan, plain, turned = peers[k]
-        scatter[k] = remote(
-            pieces.at[pl.ds(plain * held, held)], landed.at[digit], scat_send, scat_recv, k, chan
-        )
-        scatter[k].start()
 
     def tiles_of(load):
         return [load(slice(m * LANES, (m + 1) * LANES)) for m in range(count)]
@@ -170,6 +187,16 @@
         if subs > 1:
             view = target.reshape(subs // 2, 2, trials, SUB, wide)
 
+    total = pieces[pl.ds(digit * held, held)]
+    for k in rounds:
+        scatter[k].wait_recv()
+        total = total + landed[peers[k][1]]
+    gathered[pl.ds(digit * held, held)] = total * (1.0 / total_channels)
+    gather = {}
+    for k in rounds:
+        here = gathered.at[pl.ds(digit * held, held)]
+        gather[k] = remote(here, here, gath_send, gath_recv, k, peers[k][0])
+        gather[k].start()
     copies = {}
     for k in rounds:
         chan, plain, turned = peers[k]
@@ -177,21 +204,14 @@
             send.at[pl.ds(turned * held, held)], rows.at[pl.ds(digit * held, held)], row_send, row_recv, k, chan
         )
         copies[k].start()
-    own = pltpu.make_async_copy(
-        send.at[pl.ds(my_turn * held, held)], rows.at[pl.ds(digit * held, held)], own_sem
-    )
-    own.start()
-
-    total = pieces[pl.ds(digit * held, held)]
-    for k in rounds:
-        scatter[k].wait_recv()
-        total = total + landed[peers[k][1]]
-    gathered[pl.ds(digit * held, held)] = total * (1.0 / total_channels)
-    gather = {}
-    for k in rounds:
-        here = gathered.at[pl.ds(digit * held, held)]
-        gather[k] = remote(here, here, gath_send, gath_recv, k, peers[k][0])
-        gather[k].start()
+    if ending:
+        rows[pl.ds(digit * held, held)] = send[pl.ds(my_turn * held, held)]
+    else:
+        own = pltpu.make_async_copy(
+            send.at[pl.ds(my_turn * held, held)], rows.at[pl.ds(digit * held, held)], own_sem
+        )
+        own.start()
+
     for k in rounds:
         gather[k].wait_recv()
     mean = []
@@ -208,30 +228,73 @@
         for m in range(count):
             mean_row[j, :, m * LANES : (m + 1) * LANES] = line[m]
 
-    own.wait()
-    for k in rounds:
-        copies[k].wait_recv()
+    if ending:
+        dedispersed, peaks, flat = ending
+        half = mine[bits - 1]
+
+        def near():
+            for k in rounds:
+                if k < group // 2:
+                    copies[k].wait_recv()
+
+        def far():
+            for k in rounds:
+                if k >= group // 2:
+                    copies[k].wait_recv()
+
+        def keep(row, tiles):
+            for m in range(count):
+                flat[m, row * SUB : (row + 1) * SUB, :] = tiles[m]
+
+        halves = [(half * (ROWS // 2), near), ((1 - half) * (ROWS // 2), far)]
+        largest = 2 * (ROWS * group - 1) + 1
+        merge_rows(bits, 1, largest, rows, mean_row, table, my_turn, levels, keep, halves)
+        finish(length, flat, widths_in, widths, dedispersed, peaks)
+    else:
+        own.wait()
+        for k in rounds:
+            copies[k].wait_recv()
     for k in rounds:
         scatter[k].wait_send()
         gather[k].wait_send()
         copies[k].wait_send()
 
 
-def front(filterbank, shift_table, bits, total_channels):
+def front(filterbank, shift_table, box_widths, bits, total_channels, whole):
     channels, length = filterbank.shape
     wide = length // SUB
     group = 1 << bits
     held = ROWS // group
     f32 = jnp.float32
-    return pl.pallas_call(
-        functools.partial(front_kernel, bits, total_channels),
-        out_shape=(
+    vmem = pl.BlockSpec(memory_space=pltpu.VMEM)
+    if whole:
+        results = (
+            jax.ShapeDtypeStruct((ROWS, length), jnp.bfloat16),
+            jax.ShapeDtypeStruct((box_widths.shape[0], ROWS), f32),
+        )
+        places = (vmem, vmem)
+        kept = [
+            pltpu.VMEM((ROWS, SUB, wide), f32),
+            pltpu.VMEM((held, SUB, wide), f32),
+            pltpu.VMEM((wide // LANES, ROWS * SUB, LANES), f32),
+        ]
+        levels = [pltpu.VMEM((ROWS, SUB, 2 * wide), f32)] * bits
+    else:
+        results = (
             jax.ShapeDtypeStruct((ROWS, SUB, wide), f32),
             jax.ShapeDtypeStruct((held, SUB, wide), f32),
-        ),
-        in_specs=[pl.BlockSpec(memory_space=pltpu.HBM)] * 2,
-        out_specs=(pl.BlockSpec(memory_space=pl.ANY), pl.BlockSpec(memory_space=pltpu.VMEM)),
-        scratch_shapes=[
+        )
+        places = (pl.BlockSpec(memory_space=pl.ANY), vmem)
+        kept, levels = [], []
+    return pl.pallas_call(
+        functools.partial(front_kernel, bits, total_channels, whole),
+        out_shape=results,
+        in_specs=[pl.BlockSpec(memory_space=pltpu.HBM)] * 3,
+        out_specs=places,
+        scratch_shapes=kept
+        + [
+            pltpu.SMEM(box_widths.shape, box_widths.dtype),
+            pltpu.SemaphoreType.DMA,
             pltpu.VMEM(filterbank.shape, filterbank.dtype),
             pltpu.SMEM(shift_table.shape, shift_table.dtype),
             pltpu.SemaphoreType.DMA((channels // 16,)),
@@ -247,11 +310,10 @@
             pltpu.VMEM((ROWS, 2, LANES), f32),
         ]
         + [pltpu.SemaphoreType.DMA((group,))] * 6
-        + [pltpu.SemaphoreType.DMA],
-        compiler_params=pltpu.CompilerParams(
-            collective_id=0, has_side_effects=True, vmem_limit_bytes=VMEM_LIMIT
-        ),
-    )(filterbank, shift_table)
+        + [pltpu.SemaphoreType.DMA]
+        + levels,
+        compiler_params=pltpu.CompilerParams(collective_id=0, has_side_effects=True),
+    )(filterbank, shift_table, box_widths)
 
 
 def exchange_kernel(bits, stride, block, rows, row_send, row_recv, own_sem):
@@ -295,7 +357,7 @@
     )(block)
 
 
-def merge_rows(bits, merged, largest, block, correction, table_in, table, place, levels, keep):
+def merge_rows(bits, merged, largest, block, correction, table, place, levels, keep, halves):
     group = 1 << bits
     held = ROWS // group
     wide = block.shape[-1]
@@ -308,47 +370,54 @@
             return
         for m in range(count):
             levels[level][row, :, m * LANES : (m + 1) * LANES] = tiles[m]
-            if is_upper:
+            if is_upper and m * LANES < 2 * (merged * ROWS << level + 1):
                 levels[level][row, :, wide + m * LANES : wide + (m + 1) * LANES] = next_sublane(tiles[m])
 
-    for row in range(ROWS):
-        tiles = []
-        for m in range(count):
-            w = slice(m * LANES, (m + 1) * LANES)
-            tile = block[row, :, w]
-            tiles.append(tile if correction is None else tile - correction[row % held, :, w])
-        put(0, row, tiles, row // held % 2 == 1)
-    table_in.wait()
-    trials = held
-    for level in range(bits):
+    def load(base):
+        for c in range(ROWS // 2):
+            tiles = []
+            for m in range(count):
+                w = slice(m * LANES, (m + 1) * LANES)
+                tile = block[base + c, :, w]
+                tiles.append(tile if correction is None else tile - correction[c % held, :, w])
+            put(0, base + c, tiles, c // held % 2 == 1)
+
+    def run(level, base, size):
+        trials = held << level
         now = 2 * trials
         whole = merged * ROWS << level + 1
         source = levels[level]
-        pairs = [(q, i) for i in range(now) for q in range(ROWS // now)]
-        for first in range(0, ROWS, 8):
+        start = 2 * now * place
+        at = start % wide // LANES
+        pairs = [(q, i) for i in range(now) for q in range(size // now)]
+        for first in range(0, size, 8):
             made = []
             for q, i in pairs[first : first + 8]:
                 shift = table[whole - 1 + place * now + i]
-                within = shift & (wide - 1)
-                at = within // LANES
-                low = 2 * q * trials + i // 2
+                low = base + 2 * q * trials + i // 2
                 high = low + trials
                 tiles = [
                     source[high, :, pl.ds(pl.multiple_of((at + m) * LANES, LANES), LANES)]
                     for m in range(count + 1)
                 ]
-                moved = combine(tiles, within & (LANES - 1))
+                moved = combine(tiles, shift & (LANES - 1))
                 if largest >= wide:
-                    up = jnp.minimum(shift // wide, SUB)
+                    up = jnp.minimum(start // wide, SUB)
                     moved = [
                         jnp.where(sub < SUB - up, pltpu.roll(tile, (SUB - up) & (SUB - 1), 0), 0.0)
                         for tile in moved
                     ]
                 lower = [source[low, :, m * LANES : (m + 1) * LANES] for m in range(count)]
-                made.append((q * now + i, plus(lower, moved), q % 2 == 1))
+                made.append((base + q * now + i, plus(lower, moved), q % 2 == 1 or now == size))
             for row, tiles, is_upper in made:
                 put(level + 1, row, tiles, is_upper)
-        trials = now
+
+    for base, ready in halves:
+        ready()
+        load(base)
+        for level in range(bits - 1):
+            run(level, base, ROWS // 2)
+    run(bits - 1, 0, ROWS)
 
 
 def stage_position(merged, bits):
@@ -369,7 +438,8 @@
             out[row, :, m * LANES : (m + 1) * LANES] = tiles[m]
 
     place = stage_position(merged, bits)
-    merge_rows(bits, merged, largest, block, correction, table_in, table, place, levels, keep)
+    halves = [(0, table_in.wait), (ROWS // 2, lambda: None)]
+    merge_rows(bits, merged, largest, block, correction, table, place, levels, keep, halves)
 
 
 def back_kernel(bits, merged, largest, corrected, table_far, widths_far, block, *rest):
@@ -388,7 +458,13 @@
             flat[m, row * SUB : (row + 1) * SUB, :] = tiles[m]
 
     place = stage_position(merged, bits)
-    merge_rows(bits, merged, largest, block, correction, table_in, table, place, levels, keep)
+    halves = [(0, table_in.wait), (ROWS // 2, lambda: None)]
+    merge_rows(bits, merged, largest, block, correction, table, place, levels, keep, halves)
+    finish(length, flat, widths_in, widths, dedispersed, peaks)
+
+
+def finish(length, flat, widths_in, widths, dedispersed, peaks):
+    wide = length // SUB
     series = [
         jnp.concatenate([flat[m, pl.ds(s, ROWS, stride=SUB), :] for m in range(wide // LANES)], axis=1)
         for s in range(SUB)
@@ -492,7 +568,11 @@
     devices = lax.axis_size("chan")
     all_bits = devices.bit_length() - 1
     bits = min(GROUP_BITS, all_bits)
-    rows, correction = front(filterbank, shift_table, bits, filterbank.shape[0] * devices)
+    whole = bits == all_bits
+    made = front(filterbank, shift_table, box_widths, bits, filterbank.shape[0] * devices, whole)
+    if whole:
+        return made
+    rows, correction = made
     for bit in range(bits, all_bits):
         route = [(source, source ^ 1 << bit) for source in range(devices)]
         correction = correction + lax.ppermute(correction, "chan", route)

time: 23.4 us -> 24.7 us (1.056)
  Pallas kernels: 20.2 us -> 21.7 us
    pallas_call x2 -> x1, Pallas kernels: 20.2 us -> 21.7 us  [front(): pl.pallas_call(functools.partial(front_kernel, bits, total_channels, whol...]
    unnamed x6 -> x4, local copies, waits for them, and re-layouts: 2.37 us -> 2.17 us
where the time goes in v3:
time: 24.7 us; the launch traced here: 24.5 us
  Pallas kernels  21.7 us (88%)
  local copies, waits for them, and re-layouts  2.17 us (9%)
  between operations  0.65 us (3%)
    pallas_call x1, Pallas kernels, front(): pl.pallas_call(functools.partial(front_kernel, bits, total_channels, whol...  21.7 us
    unnamed x4, local copies, waits for them, and re-layouts  2.17 us

profile of v3, /device:TPU:0, one launch (start us, length us, event | category | flops | bytes accessed | tf_op | source)
XLA Modules:
  0.0 24.5 jit_solution(13069851933301160740)
XLA Ops:
  0.6 21.7 %shard_map.50 = (bf16[16,4096]{1,0:T(8,128)(2,1)}, f32[8,16]{1,0:T(8,128)}) custom-call(bf16[64,4096]{1,0:T(8,128)(2,1)} %fb_far.1, s32[511]{0:T(512)} %table_far.1, s32[8]{0:T(128)} %widths_far.1), custom_call_target="tpu_custom_call" | custom-call | tf_op jit(solution)/shard_map/pallas_call | solution.py:289
  22.4 0.0 copy-start
  22.4 1.6 %copy.7 = bf16[16,4096]{1,0:T(8,128)(2,1)} copy(bf16[16,4096]{1,0:T(8,128)(2,1)} %get-tuple-element.4) | data formatting | bytes 262144
  23.9 0.0 copy-done
  23.9 0.6 %copy.8 = f32[8,16]{1,0:T(8,128)} copy(f32[8,16]{1,0:T(8,128)S(1)} %copy-done) | data formatting | bytes 1024
Async XLA Ops:
  22.4 1.6 %copy-start = (f32[8,16]{1,0:T(8,128)S(1)}, f32[8,16]{1,0:T(8,128)}, u32[]{:S(2)}) copy-start(f32[8,16]{1,0:T(8,128)} %get-tuple-element.5) | copy-start | bytes 1540

commit v4 on v2

--- a/solution.py
+++ b/solution.py
@@ -13,8 +13,6 @@
 GROUP_BITS = 4
 
 epsilon = 1e-05
-
-VMEM_LIMIT = 48 * 1024 * 1024
 
 
 def lane_index():
@@ -119,34 +117,35 @@
                 at = s * wide + m * LANES
                 norm[m, pl.ds(first * SUB + s, step, stride=SUB), :] = scaled[:, at : at + LANES]
 
+    partial = None
+    for c in range(channels):
+        row = [norm[m, c * SUB : (c + 1) * SUB, :] for m in range(count)]
+        partial = row if partial is None else plus(partial, row)
+    for e in range(ROWS):
+        s, m = 2 * (e // count), e % count
+        pieces[e] = partial[m][s : s + 2, :]
+    if rounds:
+        pl.semaphore_wait(barrier, len(rounds))
+    scatter = {}
+    for k in rounds:
+        chan, plain, turned = peers[k]
+        scatter[k] = remote(
+            pieces.at[pl.ds(plain * held, held)], landed.at[digit], scat_send, scat_recv, k, chan
+        )
+        scatter[k].start()
+
     table_in.wait()
     single = table[0]
-    partial = None
     for q in range(channels // 4):
         row = []
         for c in range(4):
             at = (4 * q + c) * SUB
             row.append([norm[m, at : at + SUB, :] for m in range(count)])
-        summed = plus(plus(row[0], row[1]), plus(row[2], row[3]))
-        partial = summed if partial is None else plus(partial, summed)
         low = plus(row[0], advanced(row[1], single))
         high = plus(row[2], advanced(row[3], single))
         merged = plus(low, advanced(high, single))
         for m in range(count):
             base[q, :, m * LANES : (m + 1) * LANES] = merged[m]
-    for e in range(ROWS):
-        s, m = 2 * (e // count), e % count
-        pieces[e] = partial[m][s : s + 2, :]
-
-    if rounds:
-        pl.semaphore_wait(barrier, len(rounds))
-    scatter = {}
-    for k in rounds:
-        chan, plain, turned = peers[k]
-        scatter[k] = remote(
-            pieces.at[pl.ds(plain * held, held)], landed.at[digit], scat_send, scat_recv, k, chan
-        )
-        scatter[k].start()
 
     def tiles_of(load):
         return [load(slice(m * LANES, (m + 1) * LANES)) for m in range(count)]
@@ -248,9 +247,7 @@
         ]
         + [pltpu.SemaphoreType.DMA((group,))] * 6
         + [pltpu.SemaphoreType.DMA],
-        compiler_params=pltpu.CompilerParams(
-            collective_id=0, has_side_effects=True, vmem_limit_bytes=VMEM_LIMIT
-        ),
+        compiler_params=pltpu.CompilerParams(collective_id=0, has_side_effects=True),
     )(filterbank, shift_table)
 
 
@@ -290,12 +287,12 @@
         out_specs=pl.BlockSpec(memory_space=pl.ANY),
         scratch_shapes=[pltpu.SemaphoreType.DMA((group,))] * 2 + [pltpu.SemaphoreType.DMA],
         compiler_params=pltpu.CompilerParams(
-            collective_id=number, has_side_effects=True, vmem_limit_bytes=VMEM_LIMIT
+            collective_id=number, has_side_effects=True
         ),
     )(block)
 
 
-def merge_rows(bits, merged, largest, block, correction, table_in, table, place, levels, keep):
+def merge_rows(bits, merged, largest, block, correction, table, place, levels, keep, halves):
     group = 1 << bits
     held = ROWS // group
     wide = block.shape[-1]
@@ -308,47 +305,54 @@
             return
         for m in range(count):
             levels[level][row, :, m * LANES : (m + 1) * LANES] = tiles[m]
-            if is_upper:
+            if is_upper and m * LANES < 2 * (merged * ROWS << level + 1):
                 levels[level][row, :, wide + m * LANES : wide + (m + 1) * LANES] = next_sublane(tiles[m])
 
-    for row in range(ROWS):
-        tiles = []
-        for m in range(count):
-            w = slice(m * LANES, (m + 1) * LANES)
-            tile = block[row, :, w]
-            tiles.append(tile if correction is None else tile - correction[row % held, :, w])
-        put(0, row, tiles, row // held % 2 == 1)
-    table_in.wait()
-    trials = held
-    for level in range(bits):
+    def load(base):
+        for c in range(ROWS // 2):
+            tiles = []
+            for m in range(count):
+                w = slice(m * LANES, (m + 1) * LANES)
+                tile = block[base + c, :, w]
+                tiles.append(tile if correction is None else tile - correction[c % held, :, w])
+            put(0, base + c, tiles, c // held % 2 == 1)
+
+    def run(level, base, size):
+        trials = held << level
         now = 2 * trials
         whole = merged * ROWS << level + 1
         source = levels[level]
-        pairs = [(q, i) for i in range(now) for q in range(ROWS // now)]
-        for first in range(0, ROWS, 8):
+        start = 2 * now * place
+        at = start % wide // LANES
+        pairs = [(q, i) for i in range(now) for q in range(size // now)]
+        for first in range(0, size, 8):
             made = []
             for q, i in pairs[first : first + 8]:
                 shift = table[whole - 1 + place * now + i]
-                within = shift & (wide - 1)
-                at = within // LANES
-                low = 2 * q * trials + i // 2
+                low = base + 2 * q * trials + i // 2
                 high = low + trials
                 tiles = [
                     source[high, :, pl.ds(pl.multiple_of((at + m) * LANES, LANES), LANES)]
                     for m in range(count + 1)
                 ]
-                moved = combine(tiles, within & (LANES - 1))
+                moved = combine(tiles, shift & (LANES - 1))
                 if largest >= wide:
-                    up = jnp.minimum(shift // wide, SUB)
+                    up = jnp.minimum(start // wide, SUB)
                     moved = [
                         jnp.where(sub < SUB - up, pltpu.roll(tile, (SUB - up) & (SUB - 1), 0), 0.0)
                         for tile in moved
                     ]
                 lower = [source[low, :, m * LANES : (m + 1) * LANES] for m in range(count)]
-                made.append((q * now + i, plus(lower, moved), q % 2 == 1))
+                made.append((base + q * now + i, plus(lower, moved), q % 2 == 1 or now == size))
             for row, tiles, is_upper in made:
                 put(level + 1, row, tiles, is_upper)
-        trials = now
+
+    for base, ready in halves:
+        ready()
+        load(base)
+        for level in range(bits - 1):
+            run(level, base, ROWS // 2)
+    run(bits - 1, 0, ROWS)
 
 
 def stage_position(merged, bits):
@@ -369,7 +373,8 @@
             out[row, :, m * LANES : (m + 1) * LANES] = tiles[m]
 
     place = stage_position(merged, bits)
-    merge_rows(bits, merged, largest, block, correction, table_in, table, place, levels, keep)
+    halves = [(0, table_in.wait), (ROWS // 2, lambda: None)]
+    merge_rows(bits, merged, largest, block, correction, table, place, levels, keep, halves)
 
 
 def back_kernel(bits, merged, largest, corrected, table_far, widths_far, block, *rest):
@@ -388,7 +393,13 @@
             flat[m, row * SUB : (row + 1) * SUB, :] = tiles[m]
 
     place = stage_position(merged, bits)
-    merge_rows(bits, merged, largest, block, correction, table_in, table, place, levels, keep)
+    halves = [(0, table_in.wait), (ROWS // 2, lambda: None)]
+    merge_rows(bits, merged, largest, block, correction, table, place, levels, keep, halves)
+    finish(length, flat, widths_in, widths, dedispersed, peaks)
+
+
+def finish(length, flat, widths_in, widths, dedispersed, peaks):
+    wide = length // SUB
     series = [
         jnp.concatenate([flat[m, pl.ds(s, ROWS, stride=SUB), :] for m in range(wide // LANES)], axis=1)
         for s in range(SUB)
@@ -463,7 +474,7 @@
     vmem = pl.BlockSpec(memory_space=pltpu.VMEM)
     levels = [pltpu.VMEM((ROWS, SUB, 2 * wide), jnp.float32)] * bits
     table = [pltpu.SMEM(shift_table.shape, shift_table.dtype), pltpu.SemaphoreType.DMA]
-    params = pltpu.CompilerParams(vmem_limit_bytes=VMEM_LIMIT)
+    params = pltpu.CompilerParams()
     data = (block, correction) if corrected else (block,)
     if box_widths is None:
         return pl.pallas_call(

time: 23.4 us -> 22.8 us (0.974)
  local copies, waits for them, and re-layouts: 2.37 us -> 0 us
  Pallas kernels: 20.2 us -> 22 us
    unnamed x6 -> x0, local copies, waits for them, and re-layouts: 2.37 us -> none
    pallas_call x1, Pallas kernels: 3.58 us -> 4.55 us  [merge(): pl.pallas_call(functools.partial(back_kernel, bits, merged, largest, corr...]
    pallas_call x1, Pallas kernels: 16.6 us -> 17.4 us  [front(): pl.pallas_call(functools.partial(front_kernel, bits, total_channels), out...]
where the time goes in v4:
time: 22.8 us; the launch traced here: 22.6 us
  Pallas kernels  22 us (96%)
  between operations  0.64 us (3%)
    pallas_call x1, Pallas kernels, front(): pl.pallas_call(functools.partial(front_kernel, bits, total_channels), out...  17.4 us
    pallas_call x1, Pallas kernels, merge(): pl.pallas_call(functools.partial(back_kernel, bits, merged, largest, corr...  4.55 us

profile of v4, /device:TPU:0, one launch (start us, length us, event | category | flops | bytes accessed | tf_op | source)
XLA Modules:
  0.0 22.6 jit_solution(13569397448226390490)
XLA Ops:
  0.6 17.4 %shard_map.50 = (f32[16,8,512]{2,1,0:T(8,128)}, f32[1,8,512]{2,1,0:T(8,128)}) custom-call(bf16[64,4096]{1,0:T(8,128)(2,1)} %fb_far.1, s32[511]{0:T(512)} %table_far.3), custom_call_target="tpu_custom_call" | custom-call | tf_op jit(solution)/shard_map/pallas_call | solution.py:225
  18.0 4.5 %shard_map.51 = (bf16[16,4096]{1,0:T(8,128)(2,1)}, f32[8,16]{1,0:T(8,128)}) custom-call(s32[511]{0:T(512)} %table_far.3, s32[8]{0:T(128)} %widths_far.1, f32[16,8,512]{2,1,0:T(8,128)} %get-tuple-element.4.block, f32[1,8,512]{2,1,0:T(8,128)} %get-tuple-element.5.rest_0_), custom_call_target="tpu_custom_call" | custom-call | tf_op jit(solution)/shard_map/pallas_call | solution.py:489

commit v5 on v4

--- a/solution.py
+++ b/solution.py
@@ -76,7 +76,8 @@
 
 
 def front_kernel(
-    bits, total_channels, fb_far, table_far, rows, mean_row,
+    bits, total_channels, fb_far, table_far, rows, mean_far,
+    mean_row, mean_sem,
     fb, table, in_sem, table_sem, norm, base, level2, level4, level8, send, pieces, landed, gathered,
     scat_send, scat_recv, gath_send, gath_recv, row_send, row_recv, own_sem,
 ):
@@ -207,9 +208,12 @@
         for m in range(count):
             mean_row[j, :, m * LANES : (m + 1) * LANES] = line[m]
 
+    mean_out = pltpu.make_async_copy(mean_row, mean_far, mean_sem)
+    mean_out.start()
     own.wait()
     for k in rounds:
         copies[k].wait_recv()
+    mean_out.wait()
     for k in rounds:
         scatter[k].wait_send()
         gather[k].wait_send()
@@ -229,8 +233,10 @@
             jax.ShapeDtypeStruct((held, SUB, wide), f32),
         ),
         in_specs=[pl.BlockSpec(memory_space=pltpu.HBM)] * 2,
-        out_specs=(pl.BlockSpec(memory_space=pl.ANY), pl.BlockSpec(memory_space=pltpu.VMEM)),
+        out_specs=(pl.BlockSpec(memory_space=pl.ANY),) * 2,
         scratch_shapes=[
+            pltpu.VMEM((held, SUB, wide), f32),
+            pltpu.SemaphoreType.DMA,
             pltpu.VMEM(filterbank.shape, filterbank.dtype),
             pltpu.SMEM(shift_table.shape, shift_table.dtype),
             pltpu.SemaphoreType.DMA((channels // 16,)),
@@ -377,10 +383,19 @@
     merge_rows(bits, merged, largest, block, correction, table, place, levels, keep, halves)
 
 
-def back_kernel(bits, merged, largest, corrected, table_far, widths_far, block, *rest):
-    correction = rest[0] if corrected else None
-    dedispersed, peaks, flat, widths, widths_sem, table, table_sem = rest[corrected : corrected + 7]
-    levels = rest[corrected + 7 :]
+def back_kernel(bits, merged, largest, corrected, table_far, widths_far, block_far, *rest):
+    dedispersed_far, peaks, flat, widths, widths_sem, table, table_sem = rest[corrected : corrected + 7]
+    block, block_sem, dedispersed, dedispersed_sem, *levels = rest[corrected + 7 :]
+    halves_in = []
+    for n in range(2):
+        part = pl.ds(n * (ROWS // 2), ROWS // 2)
+        halves_in.append(pltpu.make_async_copy(block_far.at[part], block.at[part], block_sem.at[n]))
+        halves_in[n].start()
+    correction = None
+    if corrected:
+        correction, correction_sem, *levels = levels
+        correction_in = pltpu.make_async_copy(rest[0], correction, correction_sem)
+        correction_in.start()
     wide = block.shape[-1]
     length = wide * SUB
     table_in = pltpu.make_async_copy(table_far, table, table_sem)
@@ -393,12 +408,21 @@
             flat[m, row * SUB : (row + 1) * SUB, :] = tiles[m]
 
     place = stage_position(merged, bits)
-    halves = [(0, table_in.wait), (ROWS // 2, lambda: None)]
+
+    def first():
+        halves_in[0].wait()
+        if corrected:
+            correction_in.wait()
+        table_in.wait()
+
+    halves = [(0, first), (ROWS // 2, halves_in[1].wait)]
     merge_rows(bits, merged, largest, block, correction, table, place, levels, keep, halves)
-    finish(length, flat, widths_in, widths, dedispersed, peaks)
-
-
-def finish(length, flat, widths_in, widths, dedispersed, peaks):
+    dedispersed_out = pltpu.make_async_copy(dedispersed, dedispersed_far, dedispersed_sem)
+    finish(length, flat, widths_in, widths, dedispersed, dedispersed_out, peaks)
+    dedispersed_out.wait()
+
+
+def finish(length, flat, widths_in, widths, dedispersed, dedispersed_out, peaks):
     wide = length // SUB
     series = [
         jnp.concatenate([flat[m, pl.ds(s, ROWS, stride=SUB), :] for m in range(wide // LANES)], axis=1)
@@ -417,6 +441,7 @@
     series = [part * factor for part in series]
     for s in range(SUB):
         dedispersed[:, s * wide : (s + 1) * wide] = series[s].astype(jnp.bfloat16)
+    dedispersed_out.start()
 
     piece = 2 * LANES
     stacked = jnp.concatenate(
@@ -486,15 +511,23 @@
             compiler_params=params,
         )(shift_table, *data)
     widths = [pltpu.SMEM(box_widths.shape, box_widths.dtype), pltpu.SemaphoreType.DMA]
+    staged = [
+        pltpu.VMEM(block.shape, block.dtype),
+        pltpu.SemaphoreType.DMA((2,)),
+        pltpu.VMEM((ROWS, SUB * wide), jnp.bfloat16),
+        pltpu.SemaphoreType.DMA,
+    ]
+    if corrected:
+        staged += [pltpu.VMEM(correction.shape, correction.dtype), pltpu.SemaphoreType.DMA]
     return pl.pallas_call(
         functools.partial(back_kernel, bits, merged, largest, corrected),
         out_shape=(
             jax.ShapeDtypeStruct((ROWS, SUB * wide), jnp.bfloat16),
             jax.ShapeDtypeStruct((box_widths.shape[0], ROWS), jnp.float32),
         ),
-        in_specs=[far] * 2 + [vmem] * len(data),
-        out_specs=(vmem, vmem),
-        scratch_shapes=[pltpu.VMEM((wide // LANES, ROWS * SUB, LANES), jnp.float32)] + widths + table + levels,
+        in_specs=[far] * (2 + len(data)),
+        out_specs=(pl.BlockSpec(memory_space=pl.ANY), vmem),
+        scratch_shapes=[pltpu.VMEM((wide // LANES, ROWS * SUB, LANES), jnp.float32)] + widths + table + staged + levels,
         compiler_params=params,
     )(shift_table, box_widths, *data)
 

time: 22.8 us -> 22.3 us (0.978)
  Pallas kernels: 22 us -> 21.5 us
    pallas_call x1, Pallas kernels: 4.55 us -> 4.15 us  [merge(): pl.pallas_call(functools.partial(back_kernel, bits, merged, largest, corr...]
where the time goes in v5:
time: 22.3 us; the launch traced here: 22.2 us
  Pallas kernels  21.5 us (96%)
  between operations  0.64 us (3%)
    pallas_call x1, Pallas kernels, front(): pl.pallas_call(functools.partial(front_kernel, bits, total_channels), out...  17.4 us
    pallas_call x1, Pallas kernels, merge(): pl.pallas_call(functools.partial(back_kernel, bits, merged, largest, corr...  4.15 us

profile of v5, /device:TPU:0, one launch (start us, length us, event | category | flops | bytes accessed | tf_op | source)
XLA Modules:
  0.0 22.2 jit_solution(13146178457526073315)
XLA Ops:
  0.6 17.4 %shard_map.50 = (f32[16,8,512]{2,1,0:T(8,128)}, f32[1,8,512]{2,1,0:T(8,128)}) custom-call(bf16[64,4096]{1,0:T(8,128)(2,1)} %fb_far.1, s32[511]{0:T(512)} %table_far.3), custom_call_target="tpu_custom_call" | custom-call | tf_op jit(solution)/shard_map/pallas_call | solution.py:229
  18.0 4.1 %shard_map.51 = (bf16[16,4096]{1,0:T(8,128)(2,1)}, f32[8,16]{1,0:T(8,128)}) custom-call(s32[511]{0:T(512)} %table_far.3, s32[8]{0:T(128)} %widths_far.1, f32[16,8,512]{2,1,0:T(8,128)} %get-tuple-element.4.block_far, f32[1,8,512]{2,1,0:T(8,128)} %get-tuple-element.5.rest_0_), custom_call_target="tpu_custom_call" | custom-call | tf_op jit(solution)/shard_map/pallas_call | solution.py:522

commit v6 on v5

--- a/solution.py
+++ b/solution.py
@@ -154,7 +154,7 @@
     subs = channels // 4
     view = base.reshape(subs // 2, 2, 1, SUB, wide)
     trials = 1
-    for target in (level2, level4, level8, send):
+    for target in (level2, level4, level8):
         trials *= 2
         subs //= 2
         for i in range(trials):
@@ -163,20 +163,29 @@
             merged = plus(low, advanced(high, table[trials - 1 + i]))
             for m in range(count):
                 w = slice(m * LANES, (m + 1) * LANES)
-                if subs > 1:
-                    target[:, i, :, w] = merged[m]
-                else:
-                    target[i, :, w] = merged[m][0]
-        if subs > 1:
-            view = target.reshape(subs // 2, 2, trials, SUB, wide)
+                target[:, i, :, w] = merged[m]
+        view = target.reshape(subs // 2, 2, trials, SUB, wide)
 
     copies = {}
-    for k in rounds:
-        chan, plain, turned = peers[k]
-        copies[k] = remote(
-            send.at[pl.ds(turned * held, held)], rows.at[pl.ds(digit * held, held)], row_send, row_recv, k, chan
-        )
-        copies[k].start()
+    top = mine[bits - 1]
+    for distant, turn in ((True, 1 - top), (False, top)):
+        for a in range(group // 2):
+            for b in range(held):
+                trial = (2 * a + turn) * held + b
+                parent = a if held == 1 else trial // 2
+                low = tiles_of(lambda w: level8[0, parent, :, w])
+                high = tiles_of(lambda w: level8[1, parent, :, w])
+                merged = plus(low, advanced(high, table[ROWS - 1 + trial]))
+                for m in range(count):
+                    send[trial, :, m * LANES : (m + 1) * LANES] = merged[m]
+        for k in rounds:
+            if (k >= group // 2) == distant:
+                chan, plain, turned = peers[k]
+                copies[k] = remote(
+                    send.at[pl.ds(turned * held, held)], rows.at[pl.ds(digit * held, held)],
+                    row_send, row_recv, k, chan,
+                )
+                copies[k].start()
     own = pltpu.make_async_copy(
         send.at[pl.ds(my_turn * held, held)], rows.at[pl.ds(digit * held, held)], own_sem
     )

time: 22.3 us -> 22.2 us (level)
  no operation moved by 1% of the time
where the time goes in v6:
time: 22.2 us; the launch traced here: 22 us
  Pallas kernels  21.4 us (96%)
  between operations  0.64 us (3%)
    pallas_call x1, Pallas kernels, front(): pl.pallas_call(functools.partial(front_kernel, bits, total_channels), out...  17.2 us
    pallas_call x1, Pallas kernels, merge(): pl.pallas_call(functools.partial(back_kernel, bits, merged, largest, corr...  4.15 us

profile of v6, /device:TPU:0, one launch (start us, length us, event | category | flops | bytes accessed | tf_op | source)
XLA Modules:
  0.0 22.0 jit_solution(13569606082689429499)
XLA Ops:
  0.6 17.2 %shard_map.50 = (f32[16,8,512]{2,1,0:T(8,128)}, f32[1,8,512]{2,1,0:T(8,128)}) custom-call(bf16[64,4096]{1,0:T(8,128)(2,1)} %fb_far.1, s32[511]{0:T(512)} %table_far.3), custom_call_target="tpu_custom_call" | custom-call | tf_op jit(solution)/shard_map/pallas_call | solution.py:238
  17.9 4.1 %shard_map.51 = (bf16[16,4096]{1,0:T(8,128)(2,1)}, f32[8,16]{1,0:T(8,128)}) custom-call(s32[511]{0:T(512)} %table_far.3, s32[8]{0:T(128)} %widths_far.1, f32[16,8,512]{2,1,0:T(8,128)} %get-tuple-element.4.block_far, f32[1,8,512]{2,1,0:T(8,128)} %get-tuple-element.5.rest_0_), custom_call_target="tpu_custom_call" | custom-call | tf_op jit(solution)/shard_map/pallas_call | solution.py:531
